TPU v7x, 128 devices: a whole 4x4x4 slice. The times are simulated.
128 devices in a mesh: dap: 16 (over z, y_hi, core), ch: 8 (over y_lo, x).
Axes of the slice: x: 4, y: 4 (y_hi: 2, y_lo: 2; y = y_hi * 2 + y_lo), z: 4, core: 2. Of those that a mesh axis runs over, the one named last changes fastest.
Arguments:
- homolog_matrix_entering: bfloat16 [128, 1024, 256], P('ch', 'dap'), may hold values from -6 to 6
- attention_increment_undropped: bfloat16 [128, 1024, 256], P('ch', 'dap'), may hold values from -6 to 6
- retained_entries_indicator: int32 [1024, 256], P('dap'), may hold values 0 or 1
- pair: bfloat16 [128, 1024, 1024], P(None, 'dap', 'ch'), may hold values from -6 to 6
- pair_keep_mask: int32 [128, 1024], P(None, 'ch'), may hold values 0 or 1
- homolog_standardizing_multiplier: float32 [256], replicated, may hold values from 0.1 to 1.9
- left_right_factor_matrices: bfloat16 [256, 64], replicated, may hold values from -0.375 to 0.375
- outer_product_output_weight: bfloat16 [1024, 128], replicated, may hold values from -2 to 2
- triangle_input_gain: float32 [128], replicated, may hold values from 0.1 to 1.9
- triangle_input_weight: bfloat16 [128, 640], replicated, may hold values from -0.5 to 0.5
- triangle_output_gain: float32 [128], replicated, may hold values from 0.1 to 1.9
- triangle_output_weight: bfloat16 [128, 128], replicated, may hold values from -0.5 to 0.5
Outputs:
- pair_out: bfloat16 [128, 1024, 1024], P(None, 'dap', 'ch')
All inputs are finite; a program needn't handle non-finite values. No bound on the sum of `retained_entries_indicator` or of `pair_keep_mask` on one device may be relied on, other than what follows from the above.
Results may differ from a plain program's by a relative error of at most 0.011.
Values may be sent and summed in bfloat16 or wider, within the bound.
No kernel may reach another device: no remote copies, remote signals or barrier semaphores. Data moves between devices by JAX's collectives and lax.ppermute only.
A program may use at most 192 MiB of HBM per device.

v0:
```python
import math

import jax
import jax.numpy as jnp
from jax import lax
from jax.sharding import PartitionSpec as P


def layer_norm_trailing(values, gain):
    center = values - jnp.mean(values, axis=-1, keepdims=True)
    spread = jnp.mean(center * center, axis=-1, keepdims=True)
    return center * lax.rsqrt(spread + 1e-05) * gain


def norm_first(values, gain):
    center = values - jnp.mean(values, axis=0, keepdims=True)
    spread = jnp.mean(center * center, axis=0, keepdims=True)
    return center * lax.rsqrt(spread + 1e-05) * gain[:, None, None]


def on_device(
    homolog_matrix_entering,
    attention_increment_undropped,
    retained_entries_indicator,
    pair,
    pair_keep_mask,
    homolog_standardizing_multiplier,
    left_right_factor_matrices,
    outer_product_output_weight,
    triangle_input_gain,
    triangle_input_weight,
    triangle_output_gain,
    triangle_output_weight,
):
    sequence_total, residue_row_count, alignment_channel_width = homolog_matrix_entering.shape
    channels, _, col_count = pair.shape
    hidden = left_right_factor_matrices.shape[1] // 2
    dropout_scale = retained_entries_indicator.astype(jnp.float32) / 0.85
    alignment_residual_sum = homolog_matrix_entering.astype(jnp.float32) + dropout_scale[
        None
    ] * attention_increment_undropped.astype(jnp.float32)
    alignment_normalized = layer_norm_trailing(
        alignment_residual_sum, homolog_standardizing_multiplier
    ).astype(jnp.bfloat16)
    projected_operands = jnp.einsum(
        "ted,dx->tex",
        alignment_normalized,
        left_right_factor_matrices,
        preferred_element_type=jnp.float32,
    ).astype(jnp.bfloat16)
    left_side = projected_operands[:, :, :hidden].reshape(
        sequence_total, residue_row_count * hidden
    )
    right_side = projected_operands[:, :, hidden:].reshape(
        sequence_total, residue_row_count * hidden
    )
    right_every = lax.all_gather(right_side, "dap", axis=1, tiled=True)
    right_all = lax.all_to_all(right_every, "ch", split_axis=1, concat_axis=0, tiled=True)
    left_all = lax.all_gather(left_side, "ch", axis=0, tiled=True)
    total_seqs = left_all.shape[0]
    out_weights = outer_product_output_weight.reshape(hidden, hidden, channels)
    row_block = math.gcd(residue_row_count, 16)

    def outer_block(block_index):
        rows_part = lax.dynamic_slice_in_dim(
            left_all, block_index * (row_block * hidden), row_block * hidden, 1
        )
        outer = lax.dot_general(
            rows_part, right_all, (((0,), (0,)), ((), ())), preferred_element_type=jnp.float32
        )
        outer = (
            (outer / total_seqs).astype(jnp.bfloat16).reshape(row_block, hidden, col_count, hidden)
        )
        return jnp.einsum("icjd,cdo->oij", outer, out_weights, preferred_element_type=jnp.float32)

    blocks = lax.map(outer_block, jnp.arange(residue_row_count // row_block, dtype=jnp.int32))
    outer_mean = jnp.moveaxis(blocks, 0, 1).reshape(channels, residue_row_count, col_count)
    pair_mid = (pair.astype(jnp.float32) + outer_mean).astype(jnp.bfloat16)
    pair_normed = norm_first(pair_mid.astype(jnp.float32), triangle_input_gain).astype(jnp.bfloat16)
    mixed = jnp.einsum(
        "cij,co->oij", pair_normed, triangle_input_weight, preferred_element_type=jnp.float32
    )
    left_value, left_gate, right_value, right_gate, out_gate = jnp.split(mixed, 5, axis=0)
    left_act = (jax.nn.sigmoid(left_gate) * left_value).astype(jnp.bfloat16)
    right_act = (jax.nn.sigmoid(right_gate) * right_value).astype(jnp.bfloat16)
    gate_act = jax.nn.sigmoid(out_gate).astype(jnp.bfloat16)
    left_chan, right_chan = (
        lax.all_to_all(left_act, "ch", split_axis=0, concat_axis=2, tiled=True),
        lax.all_to_all(right_act, "ch", split_axis=0, concat_axis=2, tiled=True),
    )
    tri_part = jnp.einsum(
        "cik,cjk->cij",
        left_chan,
        lax.all_gather(right_chan, "dap", axis=1, tiled=True),
        preferred_element_type=jnp.float32,
    ).astype(jnp.bfloat16)
    tri_sum = lax.all_to_all(tri_part, "ch", split_axis=2, concat_axis=0, tiled=True)
    tri_normed = norm_first(tri_sum.astype(jnp.float32), triangle_output_gain).astype(jnp.bfloat16)
    tri_update = jnp.einsum(
        "cij,co->oij", tri_normed, triangle_output_weight, preferred_element_type=jnp.float32
    )
    pair_scale = pair_keep_mask.astype(jnp.float32) / 0.75
    result = pair_mid.astype(jnp.float32) + pair_scale[:, None, :] * (
        gate_act.astype(jnp.float32) * tri_update
    )
    return result.astype(jnp.bfloat16)


def solution(mesh):
    placed = (
        P("ch", "dap", None),
        P("ch", "dap", None),
        P("dap", None),
        P(None, "dap", "ch"),
        P(None, "ch"),
        P(),
        P(),
        P(),
        P(),
        P(),
        P(),
        P(),
    )
    return jax.shard_map(
        on_device, mesh=mesh, in_specs=placed, out_specs=P(None, "dap", "ch"), check_vma=False
    )
```

profile of v0, /device:TPU:1, one launch (start us, length us, event | category | flops | bytes accessed | tf_op | source)
XLA Modules:
  0.0 583.6 jit_solution(4020664944417258231)
XLA Ops:
  6.5 0.9 convert_multiply_fusion.1
  7.4 1.4 fusion.38
  8.9 1.6 multiply_reduce_fusion.1
  10.5 1.9 convolution_convert_fusion
  12.6 0.9 reshape.68
  13.5 48.7 %all-gather.3.cloned.1.call-done = bf16[16,32768]{1,0:T(8,128)(2,1)} async-done(((bf16[16,2048]{1,0:T(8,128)(2,1)}), bf16[16,32768]{1,0:T(8,128)(2,1)}) %all-gather.3.cloned.1.call-update) | async-done | bytes 1048592 | tf_op jit(solution)/shard_map/all_gather | solution.py:57
  62.3 2.3 copy.105
  64.6 4.0 all-to-all-start
  68.6 0.8 copy.75
  69.5 1.2 reshape.67
  70.7 2.9 copy.74
  73.6 29.0 %all_gather.9 = bf16[128,2048]{1,0:T(8,128)(2,1)S(1)} all-gather(bf16[16,2048]{1,0:T(8,128)(2,1)S(1)} %reshape.67), channel_id=1, replica_groups=mesh['dap'=16,'ch'=8] {'ch'}, dimensions={0}, use_global_device_ids=true | all-gather | bytes 589824 | tf_op jit(solution)/shard_map/all_gather | solution.py:59
  102.6 127.5 %while.10 = (s32[]{:T(128)}, f32[4,128,16,128]{1,3,2,0:T(8,128)}, s32[4]{0:T(128)S(1)}, bf16[128,2048]{1,0:T(8,128)(2,1)S(1)}, bf16[128,4096]{1,0:T(8,128)(2,1)S...) while((s32[]{:T(128)}, f32[4,128,16,128]{1,3,2,0:T(8,128)}, ...), condition=%wide.region_3.4_spmd, body=%wide.region_2.3_spmd.sunk | while | flops 1077936128 | bytes 32899776 | solution.py:76
  103.9 3.3 multiply_convert_fusion.4
  107.1 17.3 %reshape.82 = bf16[16,32,128,32]{3,2,1,0:T(8,128)(2,1)} reshape(bf16[512,4096]{1,0:T(8,128)(2,1)} %multiply_convert_fusion.4) | data formatting | bytes 8388608 | tf_op jit(solution)/shard_map/while/body/eval_jaxpr/reshape | solution.py:72
  124.4 10.1 %fusion.61 = f32[4,128,16,128]{1,3,2,0:T(8,128)} fusion(f32[4,128,16,128]{1,3,2,0:T(8,128)} %get-tuple-element.104, s32[]{:T(128)} %get-tuple-element.103, bf16[16,32,128,32]{3,2,1,0:T(8,128)(2,1)} %reshape.82, bf16[32,32,128]{2,1,0:T(8,128)(2,1)S(1)} %copy-done.7), kind=kOutput, calls=%fused_computation.2.clone.1 | convolution fusion | flops 536870912 | bytes 18088448 | tf_op jit(solution)/shard_map/while/body/eval_jaxpr/icjd,cdo->oij/dot_general | solution.py:74
  135.7 3.3 multiply_convert_fusion.4
  139.0 17.3 %reshape.82 = bf16[16,32,128,32]{3,2,1,0:T(8,128)(2,1)} reshape(bf16[512,4096]{1,0:T(8,128)(2,1)} %multiply_convert_fusion.4) | data formatting | bytes 8388608 | tf_op jit(solution)/shard_map/while/body/eval_jaxpr/reshape | solution.py:72
  156.3 10.1 %fusion.61 = f32[4,128,16,128]{1,3,2,0:T(8,128)} fusion(f32[4,128,16,128]{1,3,2,0:T(8,128)} %get-tuple-element.104, s32[]{:T(128)} %get-tuple-element.103, bf16[16,32,128,32]{3,2,1,0:T(8,128)(2,1)} %reshape.82, bf16[32,32,128]{2,1,0:T(8,128)(2,1)S(1)} %copy-done.7), kind=kOutput, calls=%fused_computation.2.clone.1 | convolution fusion | flops 536870912 | bytes 18088448 | tf_op jit(solution)/shard_map/while/body/eval_jaxpr/icjd,cdo->oij/dot_general | solution.py:74
  167.6 3.3 multiply_convert_fusion.4
  170.9 17.3 %reshape.82 = bf16[16,32,128,32]{3,2,1,0:T(8,128)(2,1)} reshape(bf16[512,4096]{1,0:T(8,128)(2,1)} %multiply_convert_fusion.4) | data formatting | bytes 8388608 | tf_op jit(solution)/shard_map/while/body/eval_jaxpr/reshape | solution.py:72
  188.2 10.1 %fusion.61 = f32[4,128,16,128]{1,3,2,0:T(8,128)} fusion(f32[4,128,16,128]{1,3,2,0:T(8,128)} %get-tuple-element.104, s32[]{:T(128)} %get-tuple-element.103, bf16[16,32,128,32]{3,2,1,0:T(8,128)(2,1)} %reshape.82, bf16[32,32,128]{2,1,0:T(8,128)(2,1)S(1)} %copy-done.7), kind=kOutput, calls=%fused_computation.2.clone.1 | convolution fusion | flops 536870912 | bytes 18088448 | tf_op jit(solution)/shard_map/while/body/eval_jaxpr/icjd,cdo->oij/dot_general | solution.py:74
  199.5 3.3 multiply_convert_fusion.4
  202.7 17.3 %reshape.82 = bf16[16,32,128,32]{3,2,1,0:T(8,128)(2,1)} reshape(bf16[512,4096]{1,0:T(8,128)(2,1)} %multiply_convert_fusion.4) | data formatting | bytes 8388608 | tf_op jit(solution)/shard_map/while/body/eval_jaxpr/reshape | solution.py:72
  220.0 10.1 %fusion.61 = f32[4,128,16,128]{1,3,2,0:T(8,128)} fusion(f32[4,128,16,128]{1,3,2,0:T(8,128)} %get-tuple-element.104, s32[]{:T(128)} %get-tuple-element.103, bf16[16,32,128,32]{3,2,1,0:T(8,128)(2,1)} %reshape.82, bf16[32,32,128]{2,1,0:T(8,128)(2,1)S(1)} %copy-done.7), kind=kOutput, calls=%fused_computation.2.clone.1 | convolution fusion | flops 536870912 | bytes 18088448 | tf_op jit(solution)/shard_map/while/body/eval_jaxpr/icjd,cdo->oij/dot_general | solution.py:74
  230.1 4.0 convert_reduce_fusion
  234.2 2.4 fusion.6
  236.6 3.5 convolution_bitcast_fusion.1
  240.1 4.5 fusion.14
  244.5 3.8 copy-done.2
  248.4 4.1 copy.81
  252.5 25.0 %all_to_all.64 = bf16[128,64,128]{2,1,0:T(8,128)(2,1)S(1)} all-to-all(bf16[128,64,128]{2,1,0:T(8,128)(2,1)} %copy.81), channel_id=1, replica_groups=mesh['dap'=16,'ch'=8] {'ch'}, dimensions={0} | all-to-all | bytes 4194304 | tf_op jit(solution)/shard_map/all_to_all | solution.py:89
  277.5 1.9 copy.104
  279.4 4.2 copy.79
  283.6 24.9 %all_to_all.65 = bf16[128,64,128]{2,1,0:T(8,128)(2,1)} all-to-all(bf16[128,64,128]{2,1,0:T(8,128)(2,1)} %copy.79), channel_id=1, replica_groups=mesh['dap'=16,'ch'=8] {'ch'}, dimensions={0} | all-to-all | bytes 4194304 | tf_op jit(solution)/shard_map/all_to_all | solution.py:88
  308.5 176.5 %all-gather.5.cloned.1.call-done = bf16[16,1024,1024]{2,1,0:T(8,128)(2,1)} async-done(((bf16[16,64,1024]{2,1,0:T(8,128)(2,1)}), bf16[16,1024,1024]{2,1,0:T(8,128)(2,1)}) %all-gather.5.cloned.1.call-update) | async-done | bytes 33554448 | tf_op jit(solution)/shard_map/all_gather | solution.py:94
  484.9 16.6 %fusion.35 = bf16[16,64,1024]{2,1,0:T(8,128)(2,1)} fusion(bf16[16,1024,1024]{2,1,0:T(8,128)(2,1)} %all-gather.5.cloned.1.call-done, bf16[8,16,8,8,128]{4,3,2,1,0:T(8,128)(2,1)} %bitcast.109), kind=kOutput, calls=%fused_computation.51 | convolution fusion | flops 2148532224 | bytes 37748736 | tf_op jit(solution)/shard_map/cik,cjk->cij/dot_general | solution.py:91
  501.6 6.2 %copy.83 = bf16[16,64,1024]{1,0,2:T(8,128)(2,1)} copy(bf16[16,64,1024]{2,1,0:T(8,128)(2,1)} %fusion.35) | data formatting | bytes 4194304 | tf_op jit(solution)/shard_map/convert_element_type | solution.py:96
  507.7 7.6 %reshape.79 = bf16[8,2,65536]{2,1,0:T(2,128)(2,1)} reshape(bf16[1024,16,64]{2,1,0:T(8,128)(2,1)} %bitcast.107) | data formatting | bytes 4194304
  515.3 4.6 all-to-all-start.3
  520.1 26.8 %all-to-all-done.3 = bf16[8,2,65536]{2,1,0:T(2,128)(2,1)} async-done(((bf16[8,2,65536]{2,1,0:T(2,128)(2,1)}), bf16[8,2,65536]{2,1,0:T(2,128)(2,1)}, u32[]{:S(2)}, u32[]{:S(2)}) %all-to-all-start.3) | async-done | bytes 2097184 | tf_op jit(solution)/shard_map/all_to_all | solution.py:97
  546.8 7.4 %reshape.80 = bf16[1024,16,64]{2,1,0:T(8,128)(2,1)} reshape(bf16[8,2,65536]{2,1,0:T(2,128)(2,1)} %all-to-all-done.3) | data formatting | bytes 4194304
  554.2 5.4 copy.84
  559.7 2.2 copy.93
  562.9 0.8 copy.85
  563.8 0.6 fusion.25
  564.5 8.1 %fusion.9 = bf16[128,64,128]{0,2,1:T(8,128)(2,1)} fusion(bf16[128,64,128]{0,2,1:T(8,128)(2,1)S(1)} %get-tuple-element.51, f32[640,64,128]{0,2,1:T(8,128)} %copy-done.2, bf16[128,64,128]{2,1,0:T(8,128)(2,1)S(1)} %fusion.25, f32[128,128]{0,1:T(8,128)S(1)} %copy.78, bf16[128,128]{1,0:T(8,128)(2,1)S(1)} %copy-done.8), kind=kOutput, calls=%fused_computation.15 | convolution fusion | flops 278921216 | bytes 10584064 | tf_op jit(solution)/shard_map/cij,co->oij/dot_general | solution.py:99
  572.6 4.1 copy.87
  (47 shorter events, 4.0 us)
Async XLA Ops:
  6.5 230.0 %copy-start = (bf16[128,640]{1,0:T(8,128)(2,1)S(1)}, bf16[128,640]{1,0:T(8,128)(2,1)}, u32[]{:S(2)}) copy-start(bf16[128,640]{1,0:T(8,128)(2,1)} %param.23) | copy-start | bytes 491524
  6.5 55.7 %all-gather.3.cloned.1.call-start = ((), (), s32[]{:S(2)}) async-start(), calls=%async_computation.4 | async-start | bytes 1114112 | tf_op jit(solution)/shard_map/all_gather | solution.py:57
  10.5 60.2 %copy-start.3 = (bf16[128,64,128]{2,1,0:T(8,128)(2,1)S(1)}, bf16[128,64,128]{2,1,0:T(8,128)(2,1)}, u32[]{:S(2)}) copy-start(bf16[128,64,128]{2,1,0:T(8,128)(2,1)} %param.17) | copy-start | bytes 6291460
  64.6 38.1 %all-to-all-start = ((bf16[16,8,4096]{2,0,1:T(8,128)(2,1)}), bf16[16,8,4096]{2,0,1:T(8,128)(2,1)S(1)}, u32[]{:S(2)}, u32[]{:S(2)}) async-start(bf16[16,8,4096]{2,0,1:T(8,128)(2,1)} %bitcast.89), calls=%async_computation | async-start | bytes 2097152 | tf_op jit(solution)/shard_map/all_to_all | solution.py:58
  68.5 416.4 %all-gather.5.cloned.1.call-start = ((), (), s32[]{:S(2)}) async-start(), calls=%async_computation.5 | async-start | bytes 35651584 | tf_op jit(solution)/shard_map/all_gather | solution.py:94
  107.1 17.3 %copy-start.7 = (bf16[32,32,128]{2,1,0:T(8,128)(2,1)S(1)}, bf16[32,32,128]{2,1,0:T(8,128)(2,1)}, u32[]{:S(2)}) copy-start(bf16[32,32,128]{2,1,0:T(8,128)(2,1)} %get-tuple-element.118) | copy-start | bytes 786436 | tf_op jit(solution)/shard_map/while
  139.0 17.3 %copy-start.7 = (bf16[32,32,128]{2,1,0:T(8,128)(2,1)S(1)}, bf16[32,32,128]{2,1,0:T(8,128)(2,1)}, u32[]{:S(2)}) copy-start(bf16[32,32,128]{2,1,0:T(8,128)(2,1)} %get-tuple-element.118) | copy-start | bytes 786436 | tf_op jit(solution)/shard_map/while
  170.9 17.3 %copy-start.7 = (bf16[32,32,128]{2,1,0:T(8,128)(2,1)S(1)}, bf16[32,32,128]{2,1,0:T(8,128)(2,1)}, u32[]{:S(2)}) copy-start(bf16[32,32,128]{2,1,0:T(8,128)(2,1)} %get-tuple-element.118) | copy-start | bytes 786436 | tf_op jit(solution)/shard_map/while
  202.7 17.3 %copy-start.7 = (bf16[32,32,128]{2,1,0:T(8,128)(2,1)S(1)}, bf16[32,32,128]{2,1,0:T(8,128)(2,1)}, u32[]{:S(2)}) copy-start(bf16[32,32,128]{2,1,0:T(8,128)(2,1)} %get-tuple-element.118) | copy-start | bytes 786436 | tf_op jit(solution)/shard_map/while
  230.1 6.5 %copy-start.5 = (f32[128]{0:T(128)S(1)}, f32[128]{0:T(128)}, u32[]{:S(2)}) copy-start(f32[128]{0:T(128)} %param.22) | copy-start | bytes 1540
  240.0 8.3 %copy-start.2 = (f32[640,64,128]{0,2,1:T(8,128)}, f32[640,64,128]{0,2,1:T(8,128)S(1)}, u32[]{:S(2)}) copy-start(f32[640,64,128]{0,2,1:T(8,128)S(1)} %convolution_bitcast_fusion.1) | copy-start | bytes 62914564
  507.7 12.2 %copy-start.4 = (s32[128,128]{1,0:T(8,128)S(1)}, s32[128,128]{1,0:T(8,128)}, u32[]{:S(2)}) copy-start(s32[128,128]{1,0:T(8,128)} %param.18) | copy-start | bytes 196612
  515.3 31.5 %all-to-all-start.3 = ((bf16[8,2,65536]{2,1,0:T(2,128)(2,1)}), bf16[8,2,65536]{2,1,0:T(2,128)(2,1)}, u32[]{:S(2)}, u32[]{:S(2)}) async-start(bf16[8,2,65536]{2,1,0:T(2,128)(2,1)} %reshape.79), calls=%async_computation.3 | async-start | bytes 4194304 | tf_op jit(solution)/shard_map/all_to_all | solution.py:97
  562.9 0.8 copy-start.6
  563.7 0.8 copy-start.8
  564.5 12.2 %copy-start.1 = (bf16[128,640]{1,0:T(8,128)(2,1)S(1)}, bf16[128,640]{1,0:T(8,128)(2,1)}, u32[]{:S(2)}) copy-start(bf16[128,640]{1,0:T(8,128)(2,1)} %param.23) | copy-start | bytes 491524
Sparse Core Ops, SparseCore 0:
  13.6 48.5 all-gather.2
  279.5 205.3 all-gather.4
where the time goes:
time: 589 us; the launch traced here: 584 us
  waiting for transfers between devices  252 us (43%)
  local copies, waits for them, and re-layouts  128 us (22%)
  matrix products  83.5 us (14%)
  blocking collectives  78.9 us (13%)
  other arithmetic  16.2 us (3%)
  between operations  13.7 us (2%)
  starting transfers between devices  8.64 us (1%)
    all_gather x1, waiting for transfers between devices, on_device(): lax.all_gather(right_chan, 'dap', axis=1, tiled=True)  176 us
    reshape x4, local copies, waits for them, and re-layouts, outer_block(): (outer / total_seqs).astype(jnp.bfloat16)  69.1 us
    all_gather x1, waiting for transfers between devices, on_device(): right_every = lax.all_gather(right_side, 'dap', axis=1, tiled=True)  48.7 us
    dot_general x4, matrix products, outer_block(): jnp.einsum('icjd,cdo->oij', outer, out_weights, preferred_element_type=jn...  40.4 us
    all_gather x1, blocking collectives, on_device(): left_all = lax.all_gather(left_side, 'ch', axis=0, tiled=True)  29 us
    all_to_all x1, waiting for transfers between devices, on_device(): lax.all_to_all(tri_part, 'ch', split_axis=2, concat_axis=0, tiled=True)  26.8 us
    all_to_all x1, blocking collectives, on_device(): lax.all_to_all(right_act, 'ch', split_axis=0, concat_axis=2, tiled=True)  25 us
    all_to_all x1, blocking collectives, on_device(): lax.all_to_all(left_act, 'ch', split_axis=0, concat_axis=2, tiled=True)  24.9 us
  transfers between devices with their start and end apart: 4, of which 3 were waited for; matrix products, arithmetic and copies ran while one was open for 2% of the time, Pallas kernels for 0%

commit v1 on v0

v1 whole, which is shorter than its diff:
```python
import jax
import jax.numpy as jnp
from jax import lax
from jax.experimental import pallas as pl
from jax.experimental.pallas import tpu as pltpu
from jax.sharding import PartitionSpec as P

F32 = jnp.float32
BF16 = jnp.bfloat16
EPS = 1e-05
VMEM_LIMIT = 56 * 1024 * 1024
HIDDEN = 32
LANES = 128
ROWS = 64
STEP_ROWS = 16
GROUP = 4


def contract_last(a, b):
    return lax.dot_general(a, b, (((1,), (1,)), ((), ())), preferred_element_type=F32)


def params():
    return pltpu.CompilerParams(vmem_limit_bytes=VMEM_LIMIT, dimension_semantics=("arbitrary",))


def operands_kernel(homolog, increment, keep, gain, weight, out, rows_out):
    step = pl.program_id(0)
    scale = keep[...].astype(F32) / 0.85
    for t in range(2):
        parts = []
        for half in range(2):
            x = homolog[half, t].astype(F32) + scale * increment[half, t].astype(F32)
            center = x - jnp.mean(x, axis=-1, keepdims=True)
            spread = jnp.mean(center * center, axis=-1, keepdims=True)
            parts.append((center * lax.rsqrt(spread + EPS) * gain[...]).astype(BF16))
        projected = contract_last(weight[...], jnp.concatenate(parts, axis=0))
        rows_out[pl.ds(step * 2 + t, 64, stride=8), :] = projected

    @pl.when(step == pl.num_programs(0) - 1)
    def _():
        out[...] = rows_out[...].astype(BF16)


def pair_kernel(
    places, l0, l1, l2, l3, r0, r1, pair, out_weight, gain, in_weight,
    acts, mid_out, gate_out,
    l_parts, r_parts, l_rows, left, right, outer, pair_rows, left_rows, right_rows,
):
    step = pl.program_id(0)

    @pl.when(step == 0)
    def _():
        for k, block in enumerate((l0, l1, l2, l3)):
            for q in range(2):
                l_parts[places[2 * k + q]] = block[q].astype(F32).reshape(HIDDEN, 8, LANES)
        for k, block in enumerate((r0, r1)):
            for q in range(8):
                r_parts[places[8 + 8 * k + q]] = block[q].astype(F32).reshape(HIDDEN, 8, LANES)
        for c in range(HIDDEN):
            turned = l_parts[:, c].reshape(64, LANES).T
            l_rows[pl.ds(c, ROWS, stride=HIDDEN), :] = jnp.concatenate([turned[:64], turned[64:]], axis=1)
        left[...] = l_rows[...].astype(BF16)
        low = lax.broadcasted_iota(jnp.int32, (64, LANES), 1) < 64
        for d in range(HIDDEN):
            a0 = r_parts[0:8, d].reshape(64, LANES)
            a1 = r_parts[8:16, d].reshape(64, LANES)
            first = jnp.where(low, a0, pltpu.roll(a1, 64, 1))
            second = jnp.where(low, pltpu.roll(a0, 64, 1), a1)
            right[:, d * LANES:(d + 1) * LANES] = jnp.concatenate([first, second], axis=0).astype(BF16)

    pair_rows[...] = pair[...].astype(F32).reshape(LANES * STEP_ROWS, LANES)
    rows = left[pl.ds(pl.multiple_of(step * (STEP_ROWS * HIDDEN), STEP_ROWS * HIDDEN), STEP_ROWS * HIDDEN), :]
    for n in range(16):
        product = jnp.dot(rows, right[:, n * 256:(n + 1) * 256], preferred_element_type=F32).astype(BF16)
        for i in range(STEP_ROWS):
            for q in range(2):
                d = 2 * n + q
                outer[d * HIDDEN:(d + 1) * HIDDEN, i * LANES:(i + 1) * LANES] = product[
                    i * HIDDEN:(i + 1) * HIDDEN, q * LANES:(q + 1) * LANES
                ]
    for g in range(STEP_ROWS // GROUP):
        mean_part = jnp.dot(
            out_weight[...], outer[:, g * GROUP * LANES:(g + 1) * GROUP * LANES], preferred_element_type=F32
        ) * (1.0 / 128.0)
        base = jnp.concatenate(
            [pair_rows[pl.ds(g * GROUP + t, LANES, stride=STEP_ROWS), :] for t in range(GROUP)], axis=1
        )
        mid = (base + mean_part).astype(BF16)
        for t in range(GROUP):
            mid_out[g * GROUP + t] = mid[:, t * LANES:(t + 1) * LANES]
        x = mid.astype(F32)
        center = x - jnp.mean(x, axis=0, keepdims=True)
        spread = jnp.mean(center * center, axis=0, keepdims=True)
        normed = (center * lax.rsqrt(spread + EPS) * gain[...]).astype(BF16)
        mixed = jnp.dot(in_weight[...], normed, preferred_element_type=F32)
        left_act = jax.nn.sigmoid(mixed[128:256]) * mixed[0:128]
        right_act = jax.nn.sigmoid(mixed[384:512]) * mixed[256:384]
        gate_act = jax.nn.sigmoid(mixed[512:640]).astype(BF16)
        for t in range(GROUP):
            i = g * GROUP + t
            lanes = slice(t * LANES, (t + 1) * LANES)
            left_rows[pl.ds(i, LANES, stride=STEP_ROWS), :] = left_act[:, lanes]
            right_rows[pl.ds(i, LANES, stride=STEP_ROWS), :] = right_act[:, lanes]
            gate_out[i] = gate_act[:, lanes]
    acts[:, 0] = left_rows[...].reshape(LANES, STEP_ROWS, LANES).astype(BF16)
    acts[:, 1] = right_rows[...].reshape(LANES, STEP_ROWS, LANES).astype(BF16)


def triangle_kernel(left_all, right_some, out, left, right):
    @pl.when(pl.program_id(0) == 0)
    def _():
        for d in range(16):
            for h in range(8):
                left[d * 64:(d + 1) * 64, h * LANES:(h + 1) * LANES] = left_all[d, h, 0]

    for d in range(4):
        for h in range(8):
            right[d * 64:(d + 1) * 64, h * LANES:(h + 1) * LANES] = right_some[d, h, 0]
    for m in range(4):
        product = contract_last(left[m * 256:(m + 1) * 256, :], right[...]).astype(BF16)
        for d in range(4):
            for h in range(2):
                out[m * 4 + d, h] = product[d * 64:(d + 1) * 64, h * LANES:(h + 1) * LANES]


def finish_kernel(tri, mid, gate, keep, gain, weight, out, tri_rows, out_rows):
    tri_rows[...] = tri[...].astype(F32).reshape(LANES * STEP_ROWS, LANES)
    scale = keep[...].astype(F32) / 0.75
    for g in range(STEP_ROWS // GROUP):
        x = jnp.concatenate(
            [tri_rows[pl.ds(g * GROUP + t, LANES, stride=STEP_ROWS), :] for t in range(GROUP)], axis=1
        )
        center = x - jnp.mean(x, axis=0, keepdims=True)
        spread = jnp.mean(center * center, axis=0, keepdims=True)
        normed = (center * lax.rsqrt(spread + EPS) * gain[...]).astype(BF16)
        update = jnp.dot(weight[...], normed, preferred_element_type=F32)
        for t in range(GROUP):
            i = g * GROUP + t
            part = update[:, t * LANES:(t + 1) * LANES]
            out_rows[pl.ds(i, LANES, stride=STEP_ROWS), :] = mid[i].astype(F32) + scale * (
                gate[i].astype(F32) * part
            )
    out[...] = out_rows[...].reshape(LANES, STEP_ROWS, LANES).astype(BF16)


def whole(shape):
    return pl.BlockSpec(shape, lambda i: (0,) * len(shape))


def on_device(
    homolog_matrix_entering,
    attention_increment_undropped,
    retained_entries_indicator,
    pair,
    pair_keep_mask,
    homolog_standardizing_multiplier,
    left_right_factor_matrices,
    outer_product_output_weight,
    triangle_input_gain,
    triangle_input_weight,
    triangle_output_gain,
    triangle_output_weight,
):
    dap, ch = lax.axis_index("dap"), lax.axis_index("ch")
    operands = pl.pallas_call(
        operands_kernel,
        grid=(4,),
        out_shape=jax.ShapeDtypeStruct((512, LANES), BF16),
        in_specs=[
            pl.BlockSpec((2, 2, ROWS, 256), lambda i: (0, i, 0, 0)),
            pl.BlockSpec((2, 2, ROWS, 256), lambda i: (0, i, 0, 0)),
            whole((ROWS, 256)),
            whole((1, 256)),
            whole((64, 256)),
        ],
        out_specs=whole((512, LANES)),
        scratch_shapes=[pltpu.VMEM((512, LANES), F32)],
        compiler_params=params(),
        name="operands",
    )(
        homolog_matrix_entering.reshape(2, 8, ROWS, 256),
        attention_increment_undropped.reshape(2, 8, ROWS, 256),
        retained_entries_indicator,
        homolog_standardizing_multiplier.reshape(1, 256),
        left_right_factor_matrices.T,
    )
    left_block, right_block = operands[None, :256], operands[None, 256:]

    both = ("dap", "ch")

    def turn(flip):
        return [(d * 8 + h, (((d % 2) * 8 + h) ^ flip) * 8 + d // 2) for d in range(16) for h in range(8)]

    r_own = lax.ppermute(right_block, both, turn(0))
    r_flip = lax.ppermute(right_block, both, turn(2))
    l_flip = lax.ppermute(left_block, "ch", [(i, i ^ 4) for i in range(8)])
    r_pair = jnp.concatenate([r_own, r_flip], axis=0)
    l_pair = jnp.concatenate([left_block, l_flip], axis=0)
    r_quads = [r_pair] + [
        lax.ppermute(r_pair, "dap", [(i, (i + 4 * k) % 16) for i in range(16)]) for k in range(1, 4)
    ]
    l_quads = [l_pair] + [
        lax.ppermute(l_pair, "ch", [(i, (i & 4) | ((i + k) & 3)) for i in range(8)]) for k in range(1, 4)
    ]
    r_half = jnp.concatenate(r_quads, axis=0)
    r_other = lax.ppermute(r_half, "dap", [(i, i ^ 1) for i in range(16)])
    places = []
    for k in range(4):
        spot = (ch & 4) | ((ch - k) & 3)
        places += [spot, spot ^ 4]
    for core in range(2):
        for k in range(4):
            spot = ((dap ^ core) - 4 * k) & 15
            places += [spot, spot ^ 2]
    places = jnp.stack(places).astype(jnp.int32)

    acts, pair_mid, gate = pl.pallas_call(
        pair_kernel,
        grid=(ROWS // STEP_ROWS,),
        out_shape=(
            jax.ShapeDtypeStruct((LANES, 2, ROWS, LANES), BF16),
            jax.ShapeDtypeStruct((ROWS, LANES, LANES), BF16),
            jax.ShapeDtypeStruct((ROWS, LANES, LANES), BF16),
        ),
        in_specs=[pl.BlockSpec(memory_space=pltpu.SMEM)]
        + [whole((2, 256, LANES))] * 4
        + [whole((8, 256, LANES))] * 2
        + [
            pl.BlockSpec((LANES, STEP_ROWS, LANES), lambda i: (0, i, 0)),
            whole((LANES, 1024)),
            whole((LANES, 1)),
            whole((640, LANES)),
        ],
        out_specs=(
            pl.BlockSpec((LANES, 2, STEP_ROWS, LANES), lambda i: (0, 0, i, 0)),
            pl.BlockSpec((STEP_ROWS, LANES, LANES), lambda i: (i, 0, 0)),
            pl.BlockSpec((STEP_ROWS, LANES, LANES), lambda i: (i, 0, 0)),
        ),
        scratch_shapes=[
            pltpu.VMEM((8, HIDDEN, 8, LANES), F32),
            pltpu.VMEM((16, HIDDEN, 8, LANES), F32),
            pltpu.VMEM((ROWS * HIDDEN, LANES), F32),
            pltpu.VMEM((ROWS * HIDDEN, LANES), BF16),
            pltpu.VMEM((LANES, HIDDEN * LANES), BF16),
            pltpu.VMEM((1024, STEP_ROWS * LANES), BF16),
            pltpu.VMEM((LANES * STEP_ROWS, LANES), F32),
            pltpu.VMEM((LANES * STEP_ROWS, LANES), F32),
            pltpu.VMEM((LANES * STEP_ROWS, LANES), F32),
        ],
        compiler_params=params(),
        name="pair_update",
    )(
        places,
        *l_quads,
        r_half,
        r_other,
        pair,
        outer_product_output_weight.reshape(HIDDEN, HIDDEN, LANES).transpose(2, 1, 0).reshape(LANES, 1024),
        triangle_input_gain.reshape(LANES, 1),
        triangle_input_weight.T,
    )
    acts = lax.all_to_all(acts.reshape(LANES, LANES, LANES), both, 0, 0, tiled=True)
    acts = acts.reshape(16, 8, 2, ROWS, LANES)

    tri = pl.pallas_call(
        triangle_kernel,
        grid=(4,),
        out_shape=jax.ShapeDtypeStruct((16, 8, ROWS, LANES), BF16),
        in_specs=[
            pl.BlockSpec((16, 8, 1, ROWS, LANES), lambda i: (0, 0, 0, 0, 0)),
            pl.BlockSpec((4, 8, 1, ROWS, LANES), lambda i: (i, 0, 1, 0, 0)),
        ],
        out_specs=pl.BlockSpec((16, 2, ROWS, LANES), lambda i: (0, i, 0, 0)),
        scratch_shapes=[pltpu.VMEM((1024, 1024), BF16), pltpu.VMEM((256, 1024), BF16)],
        compiler_params=params(),
        name="triangle",
    )(acts, acts)
    tri = lax.all_to_all(tri.reshape(LANES, ROWS, LANES), both, 0, 0, tiled=True)

    return pl.pallas_call(
        finish_kernel,
        grid=(ROWS // STEP_ROWS,),
        out_shape=jax.ShapeDtypeStruct((LANES, ROWS, LANES), BF16),
        in_specs=[
            pl.BlockSpec((LANES, STEP_ROWS, LANES), lambda i: (0, i, 0)),
            pl.BlockSpec((STEP_ROWS, LANES, LANES), lambda i: (i, 0, 0)),
            pl.BlockSpec((STEP_ROWS, LANES, LANES), lambda i: (i, 0, 0)),
            whole((LANES, LANES)),
            whole((LANES, 1)),
            whole((LANES, LANES)),
        ],
        out_specs=pl.BlockSpec((LANES, STEP_ROWS, LANES), lambda i: (0, i, 0)),
        scratch_shapes=[
            pltpu.VMEM((LANES * STEP_ROWS, LANES), F32),
            pltpu.VMEM((LANES * STEP_ROWS, LANES), F32),
        ],
        compiler_params=params(),
        name="finish",
    )(
        tri,
        pair_mid,
        gate,
        pair_keep_mask,
        triangle_output_gain.reshape(LANES, 1),
        triangle_output_weight.T,
    )


def solution(mesh):
    placed = (
        P("ch", "dap", None),
        P("ch", "dap", None),
        P("dap", None),
        P(None, "dap", "ch"),
        P(None, "ch"),
        P(),
        P(),
        P(),
        P(),
        P(),
        P(),
        P(),
    )
    return jax.shard_map(
        on_device, mesh=mesh, in_specs=placed, out_specs=P(None, "dap", "ch"), check_vma=False
    )
```

time: 589 us -> 185 us (0.31)
  waiting for transfers between devices: 252 us -> 45.8 us
  local copies, waits for them, and re-layouts: 128 us -> 7.67 us
  matrix products: 83.5 us -> 0 us
  Pallas kernels: 0 us -> 38.7 us
  starting transfers between devices: 8.64 us -> 27.9 us
  other arithmetic: 16.2 us -> 0.01 us
  blocking collectives: 78.9 us -> 64 us
  between operations: 13.7 us -> 0.14 us
    all_gather x2 -> x0, waiting for transfers between devices: 225 us -> none  [the longest x1 176 us: on_device(): lax.all_gather(right_chan, 'dap', axis=1, tiled=True)]
    dot_general x12 -> x0, matrix products: 83.5 us -> none  [the longest x4 40.4 us: outer_block(): jnp.einsum('icjd,cdo->oij', outer, out_weights, preferred_element_type=jn...]
    reshape x6 -> x3, local copies, waits for them, and re-layouts: 71.3 us -> 2.31 us  [the longest x1 0.85 us: on_device(): outer_product_output_weight.reshape(HIDDEN, HIDDEN, LANES)]
    pallas_call x0 -> x4, Pallas kernels: none -> 38.7 us  [the longest x1 21.1 us: on_device(): pl.pallas_call(pair_kernel, grid=(ROWS // STEP_ROWS,), out_shape=(jax.Sha...]
    all_gather x1 -> x0, blocking collectives: 29 us -> none  [on_device(): left_all = lax.all_gather(left_side, 'ch', axis=0, tiled=True)]
    ppermute x0 -> x10, starting transfers between devices: none -> 23 us  [the longest x1 6.89 us: on_device(): r_own = lax.ppermute(right_block, both, turn(0))]
    unnamed x20 -> x29, local copies, waits for them, and re-layouts: 24 us -> 3.74 us
    convert_element_type x6 -> x0, local copies, waits for them, and re-layouts: 19.7 us -> none  [the longest x1 6.17 us: on_device(): tri_part = jnp.einsum('cik,cjk->cij', left_chan, lax.all_gather(right_cha...]
  transfers between devices with their start and end apart: 4 -> 11, of which waited for: 3 -> 6; matrix products, arithmetic and copies ran while one was open for 2% -> 2% of each run, Pallas kernels for 0% -> 0%
where the time goes in v1:
time: 185 us; the launch traced here: 184 us
  blocking collectives  64 us (35%)
  waiting for transfers between devices  45.8 us (25%)
  Pallas kernels  38.7 us (21%)
  starting transfers between devices  27.9 us (15%)
  local copies, waits for them, and re-layouts  7.67 us (4%)
    all_to_all x1, blocking collectives, on_device(): lax.all_to_all(acts.reshape(LANES, LANES, LANES), both, 0, 0, tiled=True)  64 us
    all_to_all x1, waiting for transfers between devices, on_device(): lax.all_to_all(tri.reshape(LANES, ROWS, LANES), both, 0, 0, tiled=True)  29.1 us
    pallas_call x1, Pallas kernels, on_device(): pl.pallas_call(pair_kernel, grid=(ROWS // STEP_ROWS,), out_shape=(jax.Sha...  21.1 us
    ppermute x1, waiting for transfers between devices, on_device(): r_flip = lax.ppermute(right_block, both, turn(2))  8.42 us
    pallas_call x1, Pallas kernels, on_device(): pl.pallas_call(finish_kernel, grid=(ROWS // STEP_ROWS,), out_shape=jax.Sh...  7.23 us
    ppermute x1, starting transfers between devices, on_device(): r_own = lax.ppermute(right_block, both, turn(0))  6.89 us
    pallas_call x1, Pallas kernels, on_device(): pl.pallas_call(triangle_kernel, grid=(4,), out_shape=jax.ShapeDtypeStruct...  6.54 us
    ppermute x3, starting transfers between devices, on_device(): lax.ppermute(r_pair, 'dap', [(i, (i + 4 * k) % 16) for i in range(16)])  6 us
  transfers between devices with their start and end apart: 11, of which 6 were waited for; matrix products, arithmetic and copies ran while one was open for 2% of the time, Pallas kernels for 0%

profile of v1, /device:TPU:1, one launch (start us, length us, event | category | flops | bytes accessed | tf_op | source)
XLA Modules:
  0.0 184.2 jit_solution(13074078185375986280)
XLA Ops:
  0.0 3.8 %operands.1 = bf16[512,128]{1,0:T(8,128)(2,1)} custom-call(bf16[2,8,64,256]{3,2,1,0:T(8,128)(2,1)} %bitcast.49, bf16[2,8,64,256]{3,2,1,0:T(8,128)(2,1)} %bitcast.50, s32[64,256]{1,0:T(8,128)} %keep.2, f32[1,256]{1,0:T(1,128)} %bitcast.54, bf16[64,256]{1,0:T(8,128)(2,1)} %bitcast.53), custom_call_target="tpu_custom_call" | custom-call | tf_op jit(solution)/shard_map/operands/pallas_call | solution.py:166
  3.8 0.9 slice_bitcast_fusion
  4.7 6.9 %collective-permute-start.4 = (bf16[1,256,128]{2,1,0:T(8,128)(2,1)S(1)}, bf16[1,256,128]{2,1,0:T(8,128)(2,1)S(1)}, u32[]{:S(2)}, u32[]{:S(2)}) collective-permute-start(bf16[1,256,128]{2,1,0:T(8,128)(2,1)S(1)} %get-tuple-element.11), channel_id=1, source_target_pairs={{0,0},{1,8},{2,16},{3,24},{4,32},{5,40},{6,48},{7,56},{8,64},{9,72... | collective-permute-start | bytes 196616 | tf_op jit(solution)/shard_map/ppermute | solution.py:195
  11.6 3.2 %collective-permute-start.5 = (bf16[1,256,128]{2,1,0:T(8,128)(2,1)S(1)}, bf16[1,256,128]{2,1,0:T(8,128)(2,1)S(1)}, u32[]{:S(2)}, u32[]{:S(2)}) collective-permute-start(bf16[1,256,128]{2,1,0:T(8,128)(2,1)S(1)} %get-tuple-element.11), channel_id=1, source_target_pairs={{0,16},{1,24},{2,0},{3,8},{4,48},{5,56},{6,32},{7,40},{8,80},{9,88... | collective-permute-start | bytes 196616 | tf_op jit(solution)/shard_map/ppermute | solution.py:196
  14.8 0.0 collective-permute-done.4
  14.8 8.4 %collective-permute-done.5 = bf16[1,256,128]{2,1,0:T(8,128)(2,1)S(1)} collective-permute-done((bf16[1,256,128]{2,1,0:T(8,128)(2,1)S(1)}, bf16[1,256,128]{2,1,0:T(8,128)(2,1)S(1)}, u32[]{:S(2)}, u32[]{:S(2)}) %collective-permute-start.5) | collective-permute-done | bytes 65568 | tf_op jit(solution)/shard_map/ppermute | solution.py:196
  23.2 0.1 collective-permute-start.6
  23.3 3.9 %collective-permute-start.7 = (bf16[2,256,128]{2,1,0:T(8,128)(2,1)S(1)}, bf16[2,256,128]{2,1,0:T(8,128)(2,1)S(1)}, u32[]{:S(2)}, u32[]{:S(2)}) collective-permute-start(bf16[2,256,128]{2,1,0:T(8,128)(2,1)S(1)} %get-tuple-element.13), channel_id=1, source_target_pairs={{0,64},{8,72},{16,80},{24,88},{32,96},{40,104},{48,112},{56,120},{... | collective-permute-start | bytes 393224 | tf_op jit(solution)/shard_map/ppermute | solution.py:201
  27.3 2.0 %collective-permute-start.8 = (bf16[2,256,128]{2,1,0:T(8,128)(2,1)S(1)}, bf16[2,256,128]{2,1,0:T(8,128)(2,1)S(1)}, u32[]{:S(2)}, u32[]{:S(2)}) collective-permute-start(bf16[2,256,128]{2,1,0:T(8,128)(2,1)S(1)} %get-tuple-element.13), channel_id=1, source_target_pairs={{0,96},{8,104},{16,112},{24,120},{32,0},{40,8},{48,16},{56,24},{64... | collective-permute-start | bytes 393224 | tf_op jit(solution)/shard_map/ppermute | solution.py:201
  29.3 0.0 collective-permute-done.6
  29.3 4.0 %collective-permute-done.7 = bf16[2,256,128]{2,1,0:T(8,128)(2,1)S(1)} collective-permute-done((bf16[2,256,128]{2,1,0:T(8,128)(2,1)S(1)}, bf16[2,256,128]{2,1,0:T(8,128)(2,1)S(1)}, u32[]{:S(2)}, u32[]{:S(2)}) %collective-permute-start.7) | collective-permute-done | bytes 131104 | tf_op jit(solution)/shard_map/ppermute | solution.py:201
  33.3 0.0 collective-permute-done.8
  33.4 0.0 copy-start.1
  33.4 1.2 collective-permute-start.9
  34.6 2.0 %collective-permute-start = (bf16[1,256,128]{2,1,0:T(8,128)(2,1)S(1)}, bf16[1,256,128]{2,1,0:T(8,128)(2,1)S(1)}, u32[]{:S(2)}, u32[]{:S(2)}) collective-permute-start(bf16[1,256,128]{2,1,0:T(8,128)(2,1)S(1)} %get-tuple-element.12), channel_id=1, source_target_pairs={{0,4},{1,5},{2,6},{3,7},{4,0},{5,1},{6,2},{7,3},{8,12},{9,13},{10,... | collective-permute-start | bytes 196616 | tf_op jit(solution)/shard_map/ppermute | solution.py:197
  36.6 2.4 %collective-permute-done = bf16[1,256,128]{2,1,0:T(8,128)(2,1)S(1)} collective-permute-done((bf16[1,256,128]{2,1,0:T(8,128)(2,1)S(1)}, bf16[1,256,128]{2,1,0:T(8,128)(2,1)S(1)}, u32[]{:S(2)}, u32[]{:S(2)}) %collective-permute-start) | collective-permute-done | bytes 65568 | tf_op jit(solution)/shard_map/ppermute | solution.py:197
  39.0 0.0 copy-start.3
  39.0 0.6 collective-permute-start.1
  39.6 2.5 %collective-permute-start.2 = (bf16[2,256,128]{2,1,0:T(8,128)(2,1)S(1)}, bf16[2,256,128]{2,1,0:T(8,128)(2,1)S(1)}, u32[]{:S(2)}, u32[]{:S(2)}) collective-permute-start(bf16[2,256,128]{2,1,0:T(8,128)(2,1)S(1)} %pad_maximum_fusion.l0), channel_id=1, source_target_pairs={{0,2},{1,3},{2,0},{3,1},{4,6},{5,7},{6,4},{7,5},{8,10},{9,11},{10,... | collective-permute-start | bytes 393224 | tf_op jit(solution)/shard_map/ppermute | solution.py:204
  42.1 0.6 collective-permute-start.3
  42.7 0.0 copy-done.4
  42.7 0.1 copy.23
  42.8 0.8 copy.25.out_weight
  43.7 0.0 copy-done.5
  43.7 0.8 copy.24
  44.5 0.0 copy-done.10
  44.5 0.7 copy.26.gain
  45.2 0.6 stack.99.places
  45.8 0.0 collective-permute-done.1.l1
  45.8 0.8 collective-permute-done.2.l2
  46.6 1.1 collective-permute-done.3.l3
  47.7 0.0 collective-permute-done.9.r1
  47.7 0.0 copy-done.1
  47.7 0.0 copy-done.3
  47.7 0.0 copy-done.6
  47.7 0.0 copy-done.7
  47.7 0.6 copy-done.8
  48.4 0.2 copy-done.2
  48.6 21.1 %pair_update.1 = (bf16[128,2,64,128]{3,2,1,0:T(8,128)(2,1)}, bf16[64,128,128]{2,1,0:T(8,128)(2,1)}, bf16[64,128,128]{2,1,0:T(8,128)(2,1)}) custom-call(s32[24]{0:T(128)} %stack.99.places, bf16[2,256,128]{2,1,0:T(8,128)(2,1)} %copy-done.3, bf16[2,256,128]{2,1,0:T(8,128)(2,1)} %copy-done.6, bf16[2,256,128]{2,1,0:T(8,128)(2,1)} %copy-done.7, ...), custom_call_target="tpu_custom_call" | custom-call | tf_op jit(solution)/shard_map/pair_update/pallas_call | solution.py:218
  69.7 64.0 %all_to_all.10 = bf16[128,128,128]{2,1,0:T(8,128)(2,1)} all-to-all(bf16[128,128,128]{2,1,0:T(8,128)(2,1)} %bitcast.46), channel_id=1, replica_groups=mesh['dap'=16,'ch'=8] {'dap','ch'}, dimensions={0} | all-to-all | bytes 8388608 | tf_op jit(solution)/shard_map/all_to_all | solution.py:263
  133.7 6.5 %triangle.1 = bf16[16,8,64,128]{3,2,1,0:T(8,128)(2,1)} custom-call(bf16[16,8,2,64,128]{4,3,2,1,0:T(8,128)(2,1)} %bitcast.43, bf16[16,8,2,64,128]{4,3,2,1,0:T(8,128)(2,1)} %bitcast.44), custom_call_target="tpu_custom_call" | custom-call | tf_op jit(solution)/shard_map/triangle/pallas_call | solution.py:266
  140.2 4.9 %all-to-all-start.1 = ((bf16[128,64,128]{2,1,0:T(8,128)(2,1)}), bf16[128,64,128]{2,1,0:T(8,128)(2,1)S(1)}, u32[]{:S(2)}, u32[]{:S(2)}) async-start(bf16[128,64,128]{2,1,0:T(8,128)(2,1)} %bitcast.45), calls=%async_computation.1 | async-start | bytes 4194304 | tf_op jit(solution)/shard_map/all_to_all | solution.py:279
  145.1 0.0 copy-done.11
  145.1 0.7 copy.28.gain
  145.8 0.7 copy.27
  146.5 29.1 %all-to-all-done.1.tri = bf16[128,64,128]{2,1,0:T(8,128)(2,1)S(1)} async-done(((bf16[128,64,128]{2,1,0:T(8,128)(2,1)}), bf16[128,64,128]{2,1,0:T(8,128)(2,1)S(1)}, u32[]{:S(2)}, u32[]{:S(2)}) %all-to-all-start.1) | async-done | bytes 2097184 | tf_op jit(solution)/shard_map/all_to_all | solution.py:279
  175.6 1.3 copy-done
  176.9 7.2 %finish.1 = bf16[128,64,128]{2,1,0:T(8,128)(2,1)} custom-call(bf16[128,64,128]{2,1,0:T(8,128)(2,1)} %copy-done, bf16[64,128,128]{2,1,0:T(8,128)(2,1)} %get-tuple-element.9.mid, bf16[64,128,128]{2,1,0:T(8,128)(2,1)} %get-tuple-element.10.gate, s32[128,128]{1,0:T(8,128)} %keep.3, f32[128,1]{1,0:T(8,128)} %copy.28.gain, bf16[128,128]{1,0:T(8,128)(2,1)} %bitcast.52), custom_call_target="tpu_custom_call" | custom-call | tf_op jit(solution)/shard_map/finish/pallas_call | solution.py:281
  (17 shorter events, 0.1 us)
Async XLA Ops:
  0.0 42.7 %copy-start.4 = (bf16[1024,128]{1,0:T(8,128)(2,1)S(1)}, bf16[1024,128]{1,0:T(8,128)(2,1)}, u32[]{:S(2)}) copy-start(bf16[1024,128]{1,0:T(8,128)(2,1)} %param.19) | copy-start | bytes 786436
  0.0 43.7 %copy-start.5 = (bf16[128,640]{1,0:T(8,128)(2,1)S(1)}, bf16[128,640]{1,0:T(8,128)(2,1)}, u32[]{:S(2)}) copy-start(bf16[128,640]{1,0:T(8,128)(2,1)} %param.21) | copy-start | bytes 491524
  0.0 44.5 %copy-start.10 = (f32[128]{0:T(128)S(1)}, f32[128]{0:T(128)}, u32[]{:S(2)}) copy-start(f32[128]{0:T(128)} %param.20) | copy-start | bytes 1540
  4.7 10.1 %collective-permute-start.4 = (bf16[1,256,128]{2,1,0:T(8,128)(2,1)S(1)}, bf16[1,256,128]{2,1,0:T(8,128)(2,1)S(1)}, u32[]{:S(2)}, u32[]{:S(2)}) collective-permute-start(bf16[1,256,128]{2,1,0:T(8,128)(2,1)S(1)} %get-tuple-element.11), channel_id=1, source_target_pairs={{0,0},{1,8},{2,16},{3,24},{4,32},{5,40},{6,48},{7,56},{8,64},{9,72... | collective-permute-start | bytes 196616 | tf_op jit(solution)/shard_map/ppermute | solution.py:195
  11.6 11.6 %collective-permute-start.5 = (bf16[1,256,128]{2,1,0:T(8,128)(2,1)S(1)}, bf16[1,256,128]{2,1,0:T(8,128)(2,1)S(1)}, u32[]{:S(2)}, u32[]{:S(2)}) collective-permute-start(bf16[1,256,128]{2,1,0:T(8,128)(2,1)S(1)} %get-tuple-element.11), channel_id=1, source_target_pairs={{0,16},{1,24},{2,0},{3,8},{4,48},{5,56},{6,32},{7,40},{8,80},{9,88... | collective-permute-start | bytes 196616 | tf_op jit(solution)/shard_map/ppermute | solution.py:196
  23.2 6.0 %collective-permute-start.6 = (bf16[2,256,128]{2,1,0:T(8,128)(2,1)S(1)}, bf16[2,256,128]{2,1,0:T(8,128)(2,1)S(1)}, u32[]{:S(2)}, u32[]{:S(2)}) collective-permute-start(bf16[2,256,128]{2,1,0:T(8,128)(2,1)S(1)} %get-tuple-element.13), channel_id=1, source_target_pairs={{0,32},{8,40},{16,48},{24,56},{32,64},{40,72},{48,80},{56,88},{64,... | collective-permute-start | bytes 393224 | tf_op jit(solution)/shard_map/ppermute | solution.py:201
  23.3 10.0 %collective-permute-start.7 = (bf16[2,256,128]{2,1,0:T(8,128)(2,1)S(1)}, bf16[2,256,128]{2,1,0:T(8,128)(2,1)S(1)}, u32[]{:S(2)}, u32[]{:S(2)}) collective-permute-start(bf16[2,256,128]{2,1,0:T(8,128)(2,1)S(1)} %get-tuple-element.13), channel_id=1, source_target_pairs={{0,64},{8,72},{16,80},{24,88},{32,96},{40,104},{48,112},{56,120},{... | collective-permute-start | bytes 393224 | tf_op jit(solution)/shard_map/ppermute | solution.py:201
  27.3 6.0 %collective-permute-start.8 = (bf16[2,256,128]{2,1,0:T(8,128)(2,1)S(1)}, bf16[2,256,128]{2,1,0:T(8,128)(2,1)S(1)}, u32[]{:S(2)}, u32[]{:S(2)}) collective-permute-start(bf16[2,256,128]{2,1,0:T(8,128)(2,1)S(1)} %get-tuple-element.13), channel_id=1, source_target_pairs={{0,96},{8,104},{16,112},{24,120},{32,0},{40,8},{48,16},{56,24},{64... | collective-permute-start | bytes 393224 | tf_op jit(solution)/shard_map/ppermute | solution.py:201
  33.4 14.4 %copy-start.1 = (bf16[8,256,128]{2,1,0:T(8,128)(2,1)}, bf16[8,256,128]{2,1,0:T(8,128)(2,1)S(1)}, u32[]{:S(2)}) copy-start(bf16[8,256,128]{2,1,0:T(8,128)(2,1)S(1)} %constant_dynamic-update-slice_fusion.2.r0) | copy-start | bytes 1572868
  33.4 14.3 %collective-permute-start.9 = (bf16[8,256,128]{2,1,0:T(8,128)(2,1)S(1)}, bf16[8,256,128]{2,1,0:T(8,128)(2,1)S(1)}, u32[]{:S(2)}, u32[]{:S(2)}) collective-permute-start(bf16[8,256,128]{2,1,0:T(8,128)(2,1)S(1)} %constant_dynamic-update-slice_fusion.2.r0), channel_id=1, source_target_pairs={{0,8},{8,0},{16,24},{24,16},{32,40},{40,32},{48,56},{56,48},{64,72... | collective-permute-start | bytes 1572872 | tf_op jit(solution)/shard_map/ppermute | solution.py:207
  34.6 4.4 %collective-permute-start = (bf16[1,256,128]{2,1,0:T(8,128)(2,1)S(1)}, bf16[1,256,128]{2,1,0:T(8,128)(2,1)S(1)}, u32[]{:S(2)}, u32[]{:S(2)}) collective-permute-start(bf16[1,256,128]{2,1,0:T(8,128)(2,1)S(1)} %get-tuple-element.12), channel_id=1, source_target_pairs={{0,4},{1,5},{2,6},{3,7},{4,0},{5,1},{6,2},{7,3},{8,12},{9,13},{10,... | collective-permute-start | bytes 196616 | tf_op jit(solution)/shard_map/ppermute | solution.py:197
  39.0 8.7 %copy-start.3 = (bf16[2,256,128]{2,1,0:T(8,128)(2,1)}, bf16[2,256,128]{2,1,0:T(8,128)(2,1)S(1)}, u32[]{:S(2)}) copy-start(bf16[2,256,128]{2,1,0:T(8,128)(2,1)S(1)} %pad_maximum_fusion.l0) | copy-start | bytes 393220
  39.0 6.8 %collective-permute-start.1 = (bf16[2,256,128]{2,1,0:T(8,128)(2,1)S(1)}, bf16[2,256,128]{2,1,0:T(8,128)(2,1)S(1)}, u32[]{:S(2)}, u32[]{:S(2)}) collective-permute-start(bf16[2,256,128]{2,1,0:T(8,128)(2,1)S(1)} %pad_maximum_fusion.l0), channel_id=1, source_target_pairs={{0,1},{1,2},{2,3},{3,0},{4,5},{5,6},{6,7},{7,4},{8,9},{9,10},{10,1... | collective-permute-start | bytes 393224 | tf_op jit(solution)/shard_map/ppermute | solution.py:204
  39.6 7.0 %collective-permute-start.2 = (bf16[2,256,128]{2,1,0:T(8,128)(2,1)S(1)}, bf16[2,256,128]{2,1,0:T(8,128)(2,1)S(1)}, u32[]{:S(2)}, u32[]{:S(2)}) collective-permute-start(bf16[2,256,128]{2,1,0:T(8,128)(2,1)S(1)} %pad_maximum_fusion.l0), channel_id=1, source_target_pairs={{0,2},{1,3},{2,0},{3,1},{4,6},{5,7},{6,4},{7,5},{8,10},{9,11},{10,... | collective-permute-start | bytes 393224 | tf_op jit(solution)/shard_map/ppermute | solution.py:204
  42.1 5.6 %collective-permute-start.3 = (bf16[2,256,128]{2,1,0:T(8,128)(2,1)S(1)}, bf16[2,256,128]{2,1,0:T(8,128)(2,1)S(1)}, u32[]{:S(2)}, u32[]{:S(2)}) collective-permute-start(bf16[2,256,128]{2,1,0:T(8,128)(2,1)S(1)} %pad_maximum_fusion.l0), channel_id=1, source_target_pairs={{0,3},{1,0},{2,1},{3,2},{4,7},{5,4},{6,5},{7,6},{8,11},{9,8},{10,9... | collective-permute-start | bytes 393224 | tf_op jit(solution)/shard_map/ppermute | solution.py:204
  45.8 1.9 %copy-start.6 = (bf16[2,256,128]{2,1,0:T(8,128)(2,1)}, bf16[2,256,128]{2,1,0:T(8,128)(2,1)S(1)}, u32[]{:S(2)}) copy-start(bf16[2,256,128]{2,1,0:T(8,128)(2,1)S(1)} %collective-permute-done.1.l1) | copy-start | bytes 393220
  46.6 1.1 copy-start.7
  47.7 0.6 copy-start.8
  47.7 0.8 copy-start.2
  140.2 4.9 %copy-start.11 = (f32[128]{0:T(128)S(1)}, f32[128]{0:T(128)}, u32[]{:S(2)}) copy-start(f32[128]{0:T(128)} %param.22) | copy-start | bytes 1540
  140.2 5.6 %copy-start.9 = (bf16[128,128]{1,0:T(8,128)(2,1)S(1)}, bf16[128,128]{1,0:T(8,128)(2,1)}, u32[]{:S(2)}) copy-start(bf16[128,128]{1,0:T(8,128)(2,1)} %param.23) | copy-start | bytes 98308
  140.2 35.4 %all-to-all-start.1 = ((bf16[128,64,128]{2,1,0:T(8,128)(2,1)}), bf16[128,64,128]{2,1,0:T(8,128)(2,1)S(1)}, u32[]{:S(2)}, u32[]{:S(2)}) async-start(bf16[128,64,128]{2,1,0:T(8,128)(2,1)} %bitcast.45), calls=%async_computation.1 | async-start | bytes 4194304 | tf_op jit(solution)/shard_map/all_to_all | solution.py:279
  175.6 1.3 copy-start

commit v2 on v0

v2 whole, which is shorter than its diff:
```python
import jax
import jax.numpy as jnp
from jax import lax
from jax.experimental import pallas as pl
from jax.experimental.pallas import tpu as pltpu
from jax.sharding import PartitionSpec as P

F32 = jnp.float32
BF16 = jnp.bfloat16
EPS = 1e-05
MIB = 1024 * 1024
HIDDEN = 32
LANES = 128
ROWS = 64
STEP_ROWS = 16
PITCH = 24
GROUP = 8


def contract_last(a, b):
    return lax.dot_general(a, b, (((1,), (1,)), ((), ())), preferred_element_type=F32)


def params(mib):
    return pltpu.CompilerParams(vmem_limit_bytes=mib * MIB, dimension_semantics=("arbitrary",))


def resident(x):
    return pltpu.with_memory_space_constraint(x, pltpu.VMEM)


def in_hbm(x):
    return pltpu.with_memory_space_constraint(x, pltpu.HBM)


IN_VMEM = pl.BlockSpec(memory_space=pltpu.VMEM)


def operands_kernel(homolog, increment, keep, gain, weight, left_out, right_out, rows_out):
    step = pl.program_id(0)
    scale = keep[...].astype(F32) / 0.85
    for t in range(2):
        parts = []
        for half in range(2):
            x = homolog[half, t].astype(F32) + scale * increment[half, t].astype(F32)
            center = x - jnp.mean(x, axis=-1, keepdims=True)
            spread = jnp.mean(center * center, axis=-1, keepdims=True)
            parts.append((center * lax.rsqrt(spread + EPS) * gain[...]).astype(BF16))
        projected = contract_last(weight[...], jnp.concatenate(parts, axis=0))
        rows_out[pl.ds(step * 2 + t, 64, stride=8), :] = projected

    @pl.when(step == pl.num_programs(0) - 1)
    def _():
        left_out[...] = jnp.broadcast_to(rows_out[0:256, :].astype(BF16), (8, 256, LANES))
        right_out[...] = rows_out[256:512, :].astype(BF16)


def spread_rows(rows, values):
    for c in range(LANES):
        rows[c * PITCH:c * PITCH + STEP_ROWS, :] = values[c]


def gather_rows(rows):
    return rows[...].reshape(LANES, PITCH, LANES)[:, :STEP_ROWS].astype(BF16)


def weights_kernel(
    out_weight, in_weight, in_gain, tri_gain, tri_weight,
    out_turned, in_turned, in_column, tri_column, tri_turned,
):
    w = out_weight[...].astype(F32).reshape(HIDDEN, HIDDEN, LANES)
    for d in range(HIDDEN // 4):
        rows = jnp.concatenate([w[:, 4 * d + q, :] for q in range(4)], axis=0)
        out_turned[:, d * LANES:(d + 1) * LANES] = rows.T.astype(BF16)
    for k in range(5):
        in_turned[k * LANES:(k + 1) * LANES, :] = in_weight[:, k * LANES:(k + 1) * LANES].astype(F32).T.astype(BF16)
    tri_turned[...] = tri_weight[...].astype(F32).T.astype(BF16)
    in_column[...] = jnp.broadcast_to(in_gain[...], (8, LANES)).T[:, 0:1]
    tri_column[...] = jnp.broadcast_to(tri_gain[...], (8, LANES)).T[:, 0:1]


def pair_kernel(
    place, l_all, r_half, r_other, pair, out_weight, gain, in_weight,
    acts, mid_out, normed_out,
    l_parts, r_parts, l_rows, left, right, outer_a, outer_b, pair_rows, left_rows, right_rows, weight_here, sem,
):
    fetch = pltpu.make_async_copy(out_weight, weight_here, sem)
    fetch.start()
    for q in range(8):
        l_parts[q] = l_all[q].astype(F32).reshape(HIDDEN, 8, LANES)
        for other, blocks in enumerate((r_half, r_other)):
            spot = (((place[0] ^ other) - 4 * (q // 2)) & 15) ^ (2 * (q % 2))
            r_parts[(spot & 1) * 8 + (spot >> 1)] = blocks[q].astype(F32).reshape(HIDDEN, 8, LANES)
    for c in range(HIDDEN):
        turned = l_parts[:, c].reshape(64, LANES).T
        l_rows[pl.ds(c, ROWS, stride=HIDDEN + 8), :] = jnp.concatenate([turned[:64], turned[64:]], axis=1)
    left[...] = l_rows[...].reshape(ROWS, HIDDEN + 8, LANES)[:, :HIDDEN].reshape(ROWS * HIDDEN, LANES).astype(BF16)
    low = lax.broadcasted_iota(jnp.int32, (64, LANES), 1) < 64
    for d in range(HIDDEN):
        a0 = r_parts[0:8, d].reshape(64, LANES)
        a1 = r_parts[8:16, d].reshape(64, LANES)
        first = jnp.where(low, a0, pltpu.roll(a1, 64, 1))
        second = jnp.where(low, pltpu.roll(a0, 64, 1), a1)
        right[:, d * LANES:(d + 1) * LANES] = jnp.concatenate([first, second], axis=0).astype(BF16)

    outers = (outer_a, outer_b)
    steps = ROWS // STEP_ROWS

    def outer_product(step, chunks):
        if step >= steps:
            return
        outer = outers[step % 2]
        rows = left[step * STEP_ROWS * HIDDEN:(step + 1) * STEP_ROWS * HIDDEN, :]
        for n in chunks:
            product = jnp.dot(rows, right[:, n * 256:(n + 1) * 256], preferred_element_type=F32).astype(BF16)
            for i in range(STEP_ROWS):
                for q in range(2):
                    d = 2 * n + q
                    outer[d * HIDDEN:(d + 1) * HIDDEN, i * LANES:(i + 1) * LANES] = product[
                        i * HIDDEN:(i + 1) * HIDDEN, q * LANES:(q + 1) * LANES
                    ]

    def update(step, g):
        mean_part = jnp.dot(
            weight_here[...], outers[step % 2][:, g * GROUP * LANES:(g + 1) * GROUP * LANES],
            preferred_element_type=F32,
        ) * (1.0 / 128.0)
        base = jnp.concatenate(
            [pair_rows[pl.ds(g * GROUP + t, LANES, stride=PITCH), :] for t in range(GROUP)], axis=1
        )
        mid = (base + mean_part).astype(BF16)
        x = mid.astype(F32)
        center = x - jnp.mean(x, axis=0, keepdims=True)
        spread = jnp.mean(center * center, axis=0, keepdims=True)
        normed = (center * lax.rsqrt(spread + EPS) * gain[...]).astype(BF16)
        for t in range(GROUP):
            i = step * STEP_ROWS + g * GROUP + t
            mid_out[i] = mid[:, t * LANES:(t + 1) * LANES]
            normed_out[i] = normed[:, t * LANES:(t + 1) * LANES]
        return normed

    def activate(g, normed):
        mixed = jnp.dot(in_weight[0:512, :], normed, preferred_element_type=F32)
        left_act = jax.nn.sigmoid(mixed[128:256]) * mixed[0:128]
        right_act = jax.nn.sigmoid(mixed[384:512]) * mixed[256:384]
        for t in range(GROUP):
            i = g * GROUP + t
            lanes = slice(t * LANES, (t + 1) * LANES)
            left_rows[pl.ds(i, LANES, stride=PITCH), :] = left_act[:, lanes]
            right_rows[pl.ds(i, LANES, stride=PITCH), :] = right_act[:, lanes]

    outer_product(0, range(16))
    fetch.wait()
    groups = STEP_ROWS // GROUP
    share = 16 // (2 * groups)
    for step in range(steps):
        here = slice(step * STEP_ROWS, (step + 1) * STEP_ROWS)
        spread_rows(pair_rows, pair[:, here, :].astype(F32))
        for g in range(groups):
            normed = update(step, g)
            outer_product(step + 1, range(2 * g * share, (2 * g + 1) * share))
            activate(g, normed)
            outer_product(step + 1, range((2 * g + 1) * share, (2 * g + 2) * share))
        acts[:, 0, here, :] = gather_rows(left_rows)
        acts[:, 1, here, :] = gather_rows(right_rows)


def triangle_kernel(acts, out):
    def rows(block, side):
        return jnp.concatenate([acts[block * 8 + h, side] for h in range(8)], axis=1)

    for n in range(4):
        right = jnp.concatenate([rows(n * 4 + d, 1) for d in range(4)], axis=0)
        for m in range(4):
            left = jnp.concatenate([rows(m * 4 + d, 0) for d in range(4)], axis=0)
            product = contract_last(left, right).astype(BF16)
            for d in range(4):
                for h in range(2):
                    out[(m * 4 + d) * 8 + n * 2 + h] = product[d * 64:(d + 1) * 64, h * LANES:(h + 1) * LANES]


def finish_kernel(tri, mid, pair_normed, keep, gain, weight, gate_weight, out, tri_rows, out_rows):
    scale = keep[...].astype(F32) / 0.75
    first = pl.multiple_of(pl.program_id(0) * STEP_ROWS, STEP_ROWS)
    spread_rows(tri_rows, tri[:, pl.ds(first, STEP_ROWS), :].astype(F32))
    for g in range(STEP_ROWS // GROUP):
        x = jnp.concatenate(
            [tri_rows[pl.ds(g * GROUP + t, LANES, stride=PITCH), :] for t in range(GROUP)], axis=1
        )
        center = x - jnp.mean(x, axis=0, keepdims=True)
        spread = jnp.mean(center * center, axis=0, keepdims=True)
        normed = (center * lax.rsqrt(spread + EPS) * gain[...]).astype(BF16)
        update = jnp.dot(weight[...], normed, preferred_element_type=F32)
        gate = jnp.dot(
            gate_weight[512:640, :],
            jnp.concatenate([pair_normed[first + g * GROUP + t] for t in range(GROUP)], axis=1),
            preferred_element_type=F32,
        )
        update = jax.nn.sigmoid(gate).astype(BF16).astype(F32) * update
        for t in range(GROUP):
            i = g * GROUP + t
            out_rows[pl.ds(i, LANES, stride=PITCH), :] = (
                mid[first + i].astype(F32) + scale * update[:, t * LANES:(t + 1) * LANES]
            )
    out[...] = gather_rows(out_rows)


def whole(shape):
    return pl.BlockSpec(shape, lambda i: (0,) * len(shape))


def on_device(
    homolog_matrix_entering,
    attention_increment_undropped,
    retained_entries_indicator,
    pair,
    pair_keep_mask,
    homolog_standardizing_multiplier,
    left_right_factor_matrices,
    outer_product_output_weight,
    triangle_input_gain,
    triangle_input_weight,
    triangle_output_gain,
    triangle_output_weight,
):
    left_blocks, right_block = pl.pallas_call(
        operands_kernel,
        grid=(4,),
        out_shape=(jax.ShapeDtypeStruct((8, 256, LANES), BF16), jax.ShapeDtypeStruct((256, LANES), BF16)),
        in_specs=[
            pl.BlockSpec((2, 2, ROWS, 256), lambda i: (0, i, 0, 0)),
            pl.BlockSpec((2, 2, ROWS, 256), lambda i: (0, i, 0, 0)),
            whole((ROWS, 256)),
            whole((1, 256)),
            whole((64, 256)),
        ],
        out_specs=(whole((8, 256, LANES)), whole((256, LANES))),
        scratch_shapes=[pltpu.VMEM((512, LANES), F32)],
        compiler_params=params(16),
        name="operands",
    )(
        in_hbm(homolog_matrix_entering.reshape(2, 8, ROWS, 256)),
        in_hbm(attention_increment_undropped.reshape(2, 8, ROWS, 256)),
        in_hbm(retained_entries_indicator),
        in_hbm(homolog_standardizing_multiplier.reshape(1, 256)),
        in_hbm(left_right_factor_matrices.T),
    )
    both = ("dap", "ch")
    turn = [(d * 8 + h, (h * 2 + d % 2) * 8 + d // 2) for d in range(16) for h in range(8)]
    right_block = lax.ppermute(right_block[None], both, turn)
    raw = lax.optimization_barrier(
        (
            outer_product_output_weight,
            triangle_input_weight,
            triangle_input_gain.reshape(1, LANES),
            triangle_output_gain.reshape(1, LANES),
            triangle_output_weight,
            left_blocks,
        )
    )
    turned = pl.pallas_call(
        weights_kernel,
        out_shape=(
            jax.ShapeDtypeStruct((LANES, 1024), BF16),
            pltpu.VMEM((640, LANES), BF16),
            pltpu.VMEM((LANES, 1), F32),
            pltpu.VMEM((LANES, 1), F32),
            pltpu.VMEM((LANES, LANES), BF16),
        ),
        in_specs=[IN_VMEM] * 5,
        out_specs=(IN_VMEM,) * 5,
        compiler_params=pltpu.CompilerParams(vmem_limit_bytes=8 * MIB),
        name="weights",
    )(*[in_hbm(x) for x in raw[:5]])
    l_all = lax.all_to_all(left_blocks, "ch", 0, 0, tiled=True)
    right_block, l_all, turned = lax.optimization_barrier((right_block, l_all, turned))
    r_flip = lax.ppermute(right_block, "dap", [(i, i ^ 2) for i in range(16)])
    r_pair = jnp.concatenate([right_block, r_flip], axis=0)
    quads = [r_pair] + [lax.ppermute(r_pair, "dap", [(i, (i + 4 * k) % 16) for i in range(16)]) for k in range(1, 4)]
    r_half = jnp.concatenate(quads, axis=0)
    r_other = lax.ppermute(r_half, "dap", [(i, i ^ 1) for i in range(16)])
    out_weight, in_weight, in_gain, tri_gain, tri_weight = turned
    place = lax.axis_index("dap").astype(jnp.int32).reshape(1)

    acts, pair_mid, normed = pl.pallas_call(
        pair_kernel,
        out_shape=(
            pltpu.VMEM((LANES, 2, ROWS, LANES), BF16),
            pltpu.VMEM((ROWS, LANES, LANES), BF16),
            pltpu.VMEM((ROWS, LANES, LANES), BF16),
        ),
        in_specs=[pl.BlockSpec(memory_space=pltpu.SMEM)]
        + [IN_VMEM] * 4
        + [pl.BlockSpec(memory_space=pl.ANY)]
        + [IN_VMEM] * 2,
        out_specs=(IN_VMEM,) * 3,
        scratch_shapes=[
            pltpu.VMEM((8, HIDDEN, 8, LANES), F32),
            pltpu.VMEM((16, HIDDEN, 8, LANES), F32),
            pltpu.VMEM((ROWS * (HIDDEN + 8), LANES), F32),
            pltpu.VMEM((ROWS * HIDDEN, LANES), BF16),
            pltpu.VMEM((LANES, HIDDEN * LANES), BF16),
            pltpu.VMEM((1024, STEP_ROWS * LANES), BF16),
            pltpu.VMEM((1024, STEP_ROWS * LANES), BF16),
            pltpu.VMEM((LANES * PITCH, LANES), F32),
            pltpu.VMEM((LANES * PITCH, LANES), F32),
            pltpu.VMEM((LANES * PITCH, LANES), F32),
            pltpu.VMEM((LANES, 1024), BF16),
            pltpu.SemaphoreType.DMA,
        ],
        compiler_params=pltpu.CompilerParams(vmem_limit_bytes=28 * MIB),
        name="pair_update",
    )(
        place, resident(l_all), resident(r_half), resident(r_other), resident(pair),
        in_hbm(out_weight), resident(in_gain), resident(in_weight),
    )
    acts = lax.all_to_all(acts.reshape(LANES, LANES, LANES), both, 0, 0, tiled=True)

    tri = pl.pallas_call(
        triangle_kernel,
        out_shape=pltpu.VMEM((LANES, ROWS, LANES), BF16),
        in_specs=[IN_VMEM],
        out_specs=IN_VMEM,
        compiler_params=pltpu.CompilerParams(vmem_limit_bytes=16 * MIB),
        name="triangle",
    )(resident(acts.reshape(LANES, 2, ROWS, LANES)))
    tri = lax.all_to_all(tri, both, 0, 0, tiled=True)

    return pl.pallas_call(
        finish_kernel,
        grid=(ROWS // STEP_ROWS,),
        out_shape=jax.ShapeDtypeStruct((LANES, ROWS, LANES), BF16),
        in_specs=[IN_VMEM] * 7,
        out_specs=pl.BlockSpec((LANES, STEP_ROWS, LANES), lambda i: (0, i, 0)),
        scratch_shapes=[pltpu.VMEM((LANES * PITCH, LANES), F32)] * 2,
        compiler_params=params(20),
        name="finish",
    )(
        resident(tri), resident(pair_mid), resident(normed), pair_keep_mask,
        resident(tri_gain), resident(tri_weight), resident(in_weight),
    )


def solution(mesh):
    placed = (
        P("ch", "dap", None),
        P("ch", "dap", None),
        P("dap", None),
        P(None, "dap", "ch"),
        P(None, "ch"),
        P(),
        P(),
        P(),
        P(),
        P(),
        P(),
        P(),
    )
    return jax.shard_map(
        on_device, mesh=mesh, in_specs=placed, out_specs=P(None, "dap", "ch"), check_vma=False
    )
```

time: 589 us -> 160 us (0.27)
  waiting for transfers between devices: 252 us -> 15 us
  local copies, waits for them, and re-layouts: 128 us -> 0.81 us
  matrix products: 83.5 us -> 0 us
  Pallas kernels: 0 us -> 26.6 us
  blocking collectives: 78.9 us -> 97.7 us
  other arithmetic: 16.2 us -> 0 us
  between operations: 13.7 us -> 0.07 us
  starting transfers between devices: 8.64 us -> 19 us
    all_gather x2 -> x0, waiting for transfers between devices: 225 us -> none  [the longest x1 176 us: on_device(): lax.all_gather(right_chan, 'dap', axis=1, tiled=True)]
    dot_general x12 -> x0, matrix products: 83.5 us -> none  [the longest x4 40.4 us: outer_block(): jnp.einsum('icjd,cdo->oij', outer, out_weights, preferred_element_type=jn...]
    reshape x6 -> x0, local copies, waits for them, and re-layouts: 71.3 us -> none  [the longest x4 69.1 us: outer_block(): (outer / total_seqs).astype(jnp.bfloat16)]
    all_to_all x2, blocking collectives: 49.9 us -> 97.7 us  [the longest x1 63 us: on_device(): lax.all_to_all(acts.reshape(LANES, LANES, LANES), both, 0, 0, tiled=True)]
    all_gather x1 -> x0, blocking collectives: 29 us -> none  [on_device(): left_all = lax.all_gather(left_side, 'ch', axis=0, tiled=True)]
    pallas_call x0 -> x5, Pallas kernels: none -> 26.6 us  [the longest x1 14.1 us: on_device(): pl.pallas_call(pair_kernel, out_shape=(pltpu.VMEM((LANES, 2, ROWS, LANES)...]
    unnamed x20 -> x9, local copies, waits for them, and re-layouts: 24 us -> 0.76 us
    convert_element_type x6 -> x0, local copies, waits for them, and re-layouts: 19.7 us -> none  [the longest x1 6.17 us: on_device(): tri_part = jnp.einsum('cik,cjk->cij', left_chan, lax.all_gather(right_cha...]
  transfers between devices with their start and end apart: 4 -> 7, of which waited for: 3 -> 6; matrix products, arithmetic and copies ran while one was open for 2% -> 0% of each run, Pallas kernels for 0% -> 1%
where the time goes in v2:
time: 160 us; the launch traced here: 159 us
  blocking collectives  97.7 us (61%)
  Pallas kernels  26.6 us (17%)
  starting transfers between devices  19 us (12%)
  waiting for transfers between devices  15 us (9%)
    all_to_all x1, blocking collectives, on_device(): lax.all_to_all(acts.reshape(LANES, LANES, LANES), both, 0, 0, tiled=True)  63 us
    all_to_all x1, blocking collectives, on_device(): tri = lax.all_to_all(tri, both, 0, 0, tiled=True)  34.7 us
    pallas_call x1, Pallas kernels, on_device(): pl.pallas_call(pair_kernel, out_shape=(pltpu.VMEM((LANES, 2, ROWS, LANES)...  14.1 us
    all_to_all x1, waiting for transfers between devices, on_device(): l_all = lax.all_to_all(left_blocks, 'ch', 0, 0, tiled=True)  7.32 us
    ppermute x3, starting transfers between devices, on_device(): lax.ppermute(r_pair, 'dap', [(i, (i + 4 * k) % 16) for i in range(16)])  6.42 us
    all_to_all x1, starting transfers between devices, on_device(): l_all = lax.all_to_all(left_blocks, 'ch', 0, 0, tiled=True)  5.86 us
    pallas_call x1, Pallas kernels, on_device(): pl.pallas_call(finish_kernel, grid=(ROWS // STEP_ROWS,), out_shape=jax.Sh...  4.5 us
    pallas_call x1, Pallas kernels, on_device(): pl.pallas_call(operands_kernel, grid=(4,), out_shape=(jax.ShapeDtypeStruc...  4.07 us
  transfers between devices with their start and end apart: 7, of which 6 were waited for; matrix products, arithmetic and copies ran while one was open for 0% of the time, Pallas kernels for 1%

profile of v2, /device:TPU:1, one launch (start us, length us, event | category | flops | bytes accessed | tf_op | source)
XLA Modules:
  0.0 159.2 jit_solution(16391747583141336474)
XLA Ops:
  0.0 0.0 copy-start
  0.0 4.1 %operands.1 = (bf16[8,256,128]{2,1,0:T(8,128)(2,1)}, bf16[256,128]{1,0:T(8,128)(2,1)S(1)}) custom-call(bf16[2,8,64,256]{3,2,1,0:T(8,128)(2,1)} %bitcast.13, bf16[2,8,64,256]{3,2,1,0:T(8,128)(2,1)} %bitcast.14, s32[64,256]{1,0:T(8,128)} %keep.2, f32[1,256]{1,0:T(1,128)} %bitcast.16, bf16[64,256]{1,0:T(8,128)(2,1)} %bitcast.15), custom_call_target="tpu_custom_call" | custom-call | tf_op jit(solution)/shard_map/operands/pallas_call | solution.py:226
  4.1 5.9 %all-to-all-start = ((bf16[8,256,128]{2,1,0:T(8,128)(2,1)}), bf16[8,256,128]{2,1,0:T(8,128)(2,1)S(1)}, u32[]{:S(2)}, u32[]{:S(2)}) async-start(bf16[8,256,128]{2,1,0:T(8,128)(2,1)} %get-tuple-element.28), calls=%async_computation | async-start | bytes 1048576 | tf_op jit(solution)/shard_map/all_to_all | solution.py:275
  9.9 0.7 collective-permute-start
  10.6 1.5 weights.1
  12.1 0.0 copy-start.1
  12.1 0.7 copy-done.1
  12.8 0.0 collective-permute-done
  12.8 7.3 %all-to-all-done.l_all = bf16[8,256,128]{2,1,0:T(8,128)(2,1)S(1)} async-done(((bf16[8,256,128]{2,1,0:T(8,128)(2,1)}), bf16[8,256,128]{2,1,0:T(8,128)(2,1)S(1)}, u32[]{:S(2)}, u32[]{:S(2)}) %all-to-all-start) | async-done | bytes 524320 | tf_op jit(solution)/shard_map/all_to_all | solution.py:275
  20.1 2.6 %collective-permute-start.1 = (bf16[1,256,128]{2,1,0:T(8,128)(2,1)S(1)}, bf16[1,256,128]{2,1,0:T(8,128)(2,1)S(1)}, u32[]{:S(2)}, u32[]{:S(2)}) collective-permute-start(bf16[1,256,128]{2,1,0:T(8,128)(2,1)S(1)} %collective-permute-done), channel_id=1, source_target_pairs={{0,16},{8,24},{16,0},{24,8},{32,48},{40,56},{48,32},{56,40},{64,80... | collective-permute-start | bytes 196616 | tf_op jit(solution)/shard_map/ppermute | solution.py:277
  22.8 2.0 %collective-permute-done.1 = bf16[1,256,128]{2,1,0:T(8,128)(2,1)S(1)} collective-permute-done((bf16[1,256,128]{2,1,0:T(8,128)(2,1)S(1)}, bf16[1,256,128]{2,1,0:T(8,128)(2,1)S(1)}, u32[]{:S(2)}, u32[]{:S(2)}) %collective-permute-start.1) | collective-permute-done | bytes 65568 | tf_op jit(solution)/shard_map/ppermute | solution.py:277
  24.8 3.2 %collective-permute-start.2 = (bf16[2,256,128]{2,1,0:T(8,128)(2,1)S(1)}, bf16[2,256,128]{2,1,0:T(8,128)(2,1)S(1)}, u32[]{:S(2)}, u32[]{:S(2)}) collective-permute-start(bf16[2,256,128]{2,1,0:T(8,128)(2,1)S(1)} %get-tuple-element.49), channel_id=1, source_target_pairs={{0,32},{8,40},{16,48},{24,56},{32,64},{40,72},{48,80},{56,88},{64,... | collective-permute-start | bytes 393224 | tf_op jit(solution)/shard_map/ppermute | solution.py:279
  28.0 2.6 %collective-permute-start.3 = (bf16[2,256,128]{2,1,0:T(8,128)(2,1)S(1)}, bf16[2,256,128]{2,1,0:T(8,128)(2,1)S(1)}, u32[]{:S(2)}, u32[]{:S(2)}) collective-permute-start(bf16[2,256,128]{2,1,0:T(8,128)(2,1)S(1)} %get-tuple-element.49), channel_id=1, source_target_pairs={{0,64},{8,72},{16,80},{24,88},{32,96},{40,104},{48,112},{56,120},{... | collective-permute-start | bytes 393224 | tf_op jit(solution)/shard_map/ppermute | solution.py:279
  30.6 0.6 collective-permute-start.4
  31.2 0.6 collective-permute-done.2
  31.8 2.7 %collective-permute-done.3 = bf16[2,256,128]{2,1,0:T(8,128)(2,1)S(1)} collective-permute-done((bf16[2,256,128]{2,1,0:T(8,128)(2,1)S(1)}, bf16[2,256,128]{2,1,0:T(8,128)(2,1)S(1)}, u32[]{:S(2)}, u32[]{:S(2)}) %collective-permute-start.3) | collective-permute-done | bytes 131104 | tf_op jit(solution)/shard_map/ppermute | solution.py:279
  34.5 0.8 collective-permute-done.4
  35.3 3.5 %collective-permute-start.5 = (bf16[8,256,128]{2,1,0:T(8,128)(2,1)S(1)}, bf16[8,256,128]{2,1,0:T(8,128)(2,1)}, u32[]{:S(2)}, u32[]{:S(2)}) collective-permute-start(bf16[8,256,128]{2,1,0:T(8,128)(2,1)S(1)} %constant_dynamic-update-slice_fusion.2.r_half), channel_id=1, source_target_pairs={{0,8},{8,0},{16,24},{24,16},{32,40},{40,32},{48,56},{56,48},{64,72... | collective-permute-start | bytes 1572872 | tf_op jit(solution)/shard_map/ppermute | solution.py:281
  38.8 1.7 %collective-permute-done.5.r_other = bf16[8,256,128]{2,1,0:T(8,128)(2,1)} collective-permute-done((bf16[8,256,128]{2,1,0:T(8,128)(2,1)S(1)}, bf16[8,256,128]{2,1,0:T(8,128)(2,1)}, u32[]{:S(2)}, u32[]{:S(2)}) %collective-permute-start.5) | collective-permute-done | bytes 524320 | tf_op jit(solution)/shard_map/ppermute | solution.py:281
  40.4 0.0 copy-done
  40.4 14.1 %pair_update.1 = (bf16[128,2,64,128]{3,2,1,0:T(8,128)(2,1)S(1)}, bf16[64,128,128]{2,1,0:T(8,128)(2,1)S(1)}, bf16[64,128,128]{2,1,0:T(8,128)(2,1)S(1)}) custom-call(s32[1]{0:T(128)} %bitcast.place, bf16[8,256,128]{2,1,0:T(8,128)(2,1)S(1)} %all-to-all-done.l_all, bf16[8,256,128]{2,1,0:T(8,128)(2,1)S(1)} %constant_dynamic-update-slice_fusion.2.r_half, ...), custom_call_target="tpu_custom_call" | custom-call | tf_op jit(solution)/shard_map/pair_update/pallas_call | solution.py:285
  54.6 63.0 %all_to_all.15 = bf16[128,128,128]{2,1,0:T(8,128)(2,1)S(1)} all-to-all(bf16[128,128,128]{2,1,0:T(8,128)(2,1)S(1)} %bitcast.11), channel_id=1, replica_groups=mesh['dap'=16,'ch'=8] {'dap','ch'}, dimensions={0} | all-to-all | bytes 8388608 | tf_op jit(solution)/shard_map/all_to_all | solution.py:317
  117.5 2.4 %triangle.1 = bf16[128,64,128]{2,1,0:T(8,128)(2,1)S(1)} custom-call(bf16[128,2,64,128]{3,2,1,0:T(8,128)(2,1)S(1)} %bitcast.10), custom_call_target="tpu_custom_call" | custom-call | tf_op jit(solution)/shard_map/triangle/pallas_call | solution.py:319
  119.9 0.0 copy-start.2
  119.9 34.7 %all_to_all.16.tri = bf16[128,64,128]{2,1,0:T(8,128)(2,1)S(1)} all-to-all(bf16[128,64,128]{2,1,0:T(8,128)(2,1)S(1)} %triangle.1), channel_id=1, replica_groups=mesh['dap'=16,'ch'=8] {'dap','ch'}, dimensions={0} | all-to-all | bytes 4194304 | tf_op jit(solution)/shard_map/all_to_all | solution.py:327
  154.7 0.0 copy-done.2
  154.7 4.5 %finish.1 = bf16[128,64,128]{2,1,0:T(8,128)(2,1)} custom-call(bf16[128,64,128]{2,1,0:T(8,128)(2,1)S(1)} %all_to_all.16.tri, bf16[64,128,128]{2,1,0:T(8,128)(2,1)S(1)} %get-tuple-element.45.mid, bf16[64,128,128]{2,1,0:T(8,128)(2,1)S(1)} %get-tuple-element.46.pair_normed, s32[128,128]{1,0:T(8,128)S(1)} %copy-done.2, f32[128,1]{1,0:T(8,128)S(1)} %get-tuple-element.47.gain, ...), custom_call_target="tpu_custom_call" | custom-call | tf_op jit(solution)/shard_map/finish/pallas_call | solution.py:329
  (5 shorter events, 0.1 us)
Async XLA Ops:
  0.0 40.4 %copy-start = (bf16[128,64,128]{2,1,0:T(8,128)(2,1)S(1)}, bf16[128,64,128]{2,1,0:T(8,128)(2,1)}, u32[]{:S(2)}) copy-start(bf16[128,64,128]{2,1,0:T(8,128)(2,1)} %pair.1) | copy-start | bytes 6291460
  4.1 16.0 %all-to-all-start = ((bf16[8,256,128]{2,1,0:T(8,128)(2,1)}), bf16[8,256,128]{2,1,0:T(8,128)(2,1)S(1)}, u32[]{:S(2)}, u32[]{:S(2)}) async-start(bf16[8,256,128]{2,1,0:T(8,128)(2,1)} %get-tuple-element.28), calls=%async_computation | async-start | bytes 1048576 | tf_op jit(solution)/shard_map/all_to_all | solution.py:275
  9.9 2.9 %collective-permute-start = (bf16[1,256,128]{2,1,0:T(8,128)(2,1)S(1)}, bf16[1,256,128]{2,1,0:T(8,128)(2,1)S(1)}, u32[]{:S(2)}, u32[]{:S(2)}) collective-permute-start(bf16[1,256,128]{2,1,0:T(8,128)(2,1)S(1)} %bitcast.12), channel_id=1, source_target_pairs={{0,0},{1,16},{2,32},{3,48},{4,64},{5,80},{6,96},{7,112},{8,8},{9,2... | collective-permute-start | bytes 196616 | tf_op jit(solution)/shard_map/ppermute | solution.py:250
  12.1 0.7 copy-start.1
  20.1 4.6 %collective-permute-start.1 = (bf16[1,256,128]{2,1,0:T(8,128)(2,1)S(1)}, bf16[1,256,128]{2,1,0:T(8,128)(2,1)S(1)}, u32[]{:S(2)}, u32[]{:S(2)}) collective-permute-start(bf16[1,256,128]{2,1,0:T(8,128)(2,1)S(1)} %collective-permute-done), channel_id=1, source_target_pairs={{0,16},{8,24},{16,0},{24,8},{32,48},{40,56},{48,32},{56,40},{64,80... | collective-permute-start | bytes 196616 | tf_op jit(solution)/shard_map/ppermute | solution.py:277
  24.8 7.0 %collective-permute-start.2 = (bf16[2,256,128]{2,1,0:T(8,128)(2,1)S(1)}, bf16[2,256,128]{2,1,0:T(8,128)(2,1)S(1)}, u32[]{:S(2)}, u32[]{:S(2)}) collective-permute-start(bf16[2,256,128]{2,1,0:T(8,128)(2,1)S(1)} %get-tuple-element.49), channel_id=1, source_target_pairs={{0,32},{8,40},{16,48},{24,56},{32,64},{40,72},{48,80},{56,88},{64,... | collective-permute-start | bytes 393224 | tf_op jit(solution)/shard_map/ppermute | solution.py:279
  28.0 6.5 %collective-permute-start.3 = (bf16[2,256,128]{2,1,0:T(8,128)(2,1)S(1)}, bf16[2,256,128]{2,1,0:T(8,128)(2,1)S(1)}, u32[]{:S(2)}, u32[]{:S(2)}) collective-permute-start(bf16[2,256,128]{2,1,0:T(8,128)(2,1)S(1)} %get-tuple-element.49), channel_id=1, source_target_pairs={{0,64},{8,72},{16,80},{24,88},{32,96},{40,104},{48,112},{56,120},{... | collective-permute-start | bytes 393224 | tf_op jit(solution)/shard_map/ppermute | solution.py:279
  30.6 4.7 %collective-permute-start.4 = (bf16[2,256,128]{2,1,0:T(8,128)(2,1)S(1)}, bf16[2,256,128]{2,1,0:T(8,128)(2,1)S(1)}, u32[]{:S(2)}, u32[]{:S(2)}) collective-permute-start(bf16[2,256,128]{2,1,0:T(8,128)(2,1)S(1)} %get-tuple-element.49), channel_id=1, source_target_pairs={{0,96},{8,104},{16,112},{24,120},{32,0},{40,8},{48,16},{56,24},{64... | collective-permute-start | bytes 393224 | tf_op jit(solution)/shard_map/ppermute | solution.py:279
  35.3 5.1 %collective-permute-start.5 = (bf16[8,256,128]{2,1,0:T(8,128)(2,1)S(1)}, bf16[8,256,128]{2,1,0:T(8,128)(2,1)}, u32[]{:S(2)}, u32[]{:S(2)}) collective-permute-start(bf16[8,256,128]{2,1,0:T(8,128)(2,1)S(1)} %constant_dynamic-update-slice_fusion.2.r_half), channel_id=1, source_target_pairs={{0,8},{8,0},{16,24},{24,16},{32,40},{40,32},{48,56},{56,48},{64,72... | collective-permute-start | bytes 1572872 | tf_op jit(solution)/shard_map/ppermute | solution.py:281
  119.9 34.8 %copy-start.2 = (s32[128,128]{1,0:T(8,128)S(1)}, s32[128,128]{1,0:T(8,128)}, u32[]{:S(2)}) copy-start(s32[128,128]{1,0:T(8,128)} %keep.3) | copy-start | bytes 196612

commit v3 on v2

--- a/solution.py
+++ b/solution.py
@@ -39,7 +39,7 @@
 def operands_kernel(homolog, increment, keep, gain, weight, left_out, right_out, rows_out):
     step = pl.program_id(0)
     scale = keep[...].astype(F32) / 0.85
-    for t in range(2):
+    for t in range(4):
         parts = []
         for half in range(2):
             x = homolog[half, t].astype(F32) + scale * increment[half, t].astype(F32)
@@ -47,11 +47,11 @@
             spread = jnp.mean(center * center, axis=-1, keepdims=True)
             parts.append((center * lax.rsqrt(spread + EPS) * gain[...]).astype(BF16))
         projected = contract_last(weight[...], jnp.concatenate(parts, axis=0))
-        rows_out[pl.ds(step * 2 + t, 64, stride=8), :] = projected
+        rows_out[pl.ds(step * 4 + t, 64, stride=8), :] = projected
 
     @pl.when(step == pl.num_programs(0) - 1)
     def _():
-        left_out[...] = jnp.broadcast_to(rows_out[0:256, :].astype(BF16), (8, 256, LANES))
+        left_out[...] = rows_out[0:256, :].astype(BF16)
         right_out[...] = rows_out[256:512, :].astype(BF16)
 
 
@@ -79,22 +79,32 @@
     tri_column[...] = jnp.broadcast_to(tri_gain[...], (8, LANES)).T[:, 0:1]
 
 
+def turn_left(place, quads, left, parts, rows):
+    for k, blocks in enumerate(quads):
+        for q in range(2):
+            spot = ((place[1] & 4) | ((place[1] - k) & 3)) ^ (4 * q)
+            parts[spot] = blocks[q].astype(F32).reshape(HIDDEN, 8, LANES)
+    for c in range(HIDDEN):
+        turned = parts[:, c].reshape(64, LANES).T
+        rows[pl.ds(c, ROWS, stride=HIDDEN + 8), :] = jnp.concatenate([turned[:64], turned[64:]], axis=1)
+    left[...] = rows[...].reshape(ROWS, HIDDEN + 8, LANES)[:, :HIDDEN].reshape(ROWS * HIDDEN, LANES).astype(BF16)
+
+
 def pair_kernel(
-    place, l_all, r_half, r_other, pair, out_weight, gain, in_weight,
+    place, l0, l1, l2, l3, r_half, r_other, pair_far, out_weight, gain, in_weight,
     acts, mid_out, normed_out,
-    l_parts, r_parts, l_rows, left, right, outer_a, outer_b, pair_rows, left_rows, right_rows, weight_here, sem,
+    l_parts, l_rows, left, r_parts, right, outer_a, outer_b, pair_rows, left_rows, right_rows,
+    weight_here, pair, weight_sem, pair_sem,
 ):
-    fetch = pltpu.make_async_copy(out_weight, weight_here, sem)
-    fetch.start()
+    fetch_weight = pltpu.make_async_copy(out_weight, weight_here, weight_sem)
+    fetch_pair = pltpu.make_async_copy(pair_far, pair, pair_sem)
+    fetch_weight.start()
+    fetch_pair.start()
+    turn_left(place, (l0, l1, l2, l3), left, l_parts, l_rows)
     for q in range(8):
-        l_parts[q] = l_all[q].astype(F32).reshape(HIDDEN, 8, LANES)
         for other, blocks in enumerate((r_half, r_other)):
             spot = (((place[0] ^ other) - 4 * (q // 2)) & 15) ^ (2 * (q % 2))
             r_parts[(spot & 1) * 8 + (spot >> 1)] = blocks[q].astype(F32).reshape(HIDDEN, 8, LANES)
-    for c in range(HIDDEN):
-        turned = l_parts[:, c].reshape(64, LANES).T
-        l_rows[pl.ds(c, ROWS, stride=HIDDEN + 8), :] = jnp.concatenate([turned[:64], turned[64:]], axis=1)
-    left[...] = l_rows[...].reshape(ROWS, HIDDEN + 8, LANES)[:, :HIDDEN].reshape(ROWS * HIDDEN, LANES).astype(BF16)
     low = lax.broadcasted_iota(jnp.int32, (64, LANES), 1) < 64
     for d in range(HIDDEN):
         a0 = r_parts[0:8, d].reshape(64, LANES)
@@ -150,7 +160,8 @@
             right_rows[pl.ds(i, LANES, stride=PITCH), :] = right_act[:, lanes]
 
     outer_product(0, range(16))
-    fetch.wait()
+    fetch_weight.wait()
+    fetch_pair.wait()
     groups = STEP_ROWS // GROUP
     share = 16 // (2 * groups)
     for step in range(steps):
@@ -223,18 +234,18 @@
     triangle_output_gain,
     triangle_output_weight,
 ):
-    left_blocks, right_block = pl.pallas_call(
+    left_block, right_block = pl.pallas_call(
         operands_kernel,
-        grid=(4,),
-        out_shape=(jax.ShapeDtypeStruct((8, 256, LANES), BF16), jax.ShapeDtypeStruct((256, LANES), BF16)),
+        grid=(2,),
+        out_shape=(jax.ShapeDtypeStruct((256, LANES), BF16), jax.ShapeDtypeStruct((256, LANES), BF16)),
         in_specs=[
-            pl.BlockSpec((2, 2, ROWS, 256), lambda i: (0, i, 0, 0)),
-            pl.BlockSpec((2, 2, ROWS, 256), lambda i: (0, i, 0, 0)),
+            pl.BlockSpec((2, 4, ROWS, 256), lambda i: (0, i, 0, 0)),
+            pl.BlockSpec((2, 4, ROWS, 256), lambda i: (0, i, 0, 0)),
             whole((ROWS, 256)),
             whole((1, 256)),
             whole((64, 256)),
         ],
-        out_specs=(whole((8, 256, LANES)), whole((256, LANES))),
+        out_specs=(whole((256, LANES)), whole((256, LANES))),
         scratch_shapes=[pltpu.VMEM((512, LANES), F32)],
         compiler_params=params(16),
         name="operands",
@@ -255,7 +266,7 @@
             triangle_input_gain.reshape(1, LANES),
             triangle_output_gain.reshape(1, LANES),
             triangle_output_weight,
-            left_blocks,
+            left_block,
         )
     )
     turned = pl.pallas_call(
@@ -272,16 +283,20 @@
         compiler_params=pltpu.CompilerParams(vmem_limit_bytes=8 * MIB),
         name="weights",
     )(*[in_hbm(x) for x in raw[:5]])
-    l_all = lax.all_to_all(left_blocks, "ch", 0, 0, tiled=True)
-    right_block, l_all, turned = lax.optimization_barrier((right_block, l_all, turned))
+    l_flip = lax.ppermute(left_block[None], "ch", [(i, i ^ 4) for i in range(8)])
+    right_block, l_flip, turned = lax.optimization_barrier((right_block, l_flip, turned))
     r_flip = lax.ppermute(right_block, "dap", [(i, i ^ 2) for i in range(16)])
+    l_pair = jnp.concatenate([left_block[None], l_flip], axis=0)
+    l_quads = [l_pair] + [
+        lax.ppermute(l_pair, "ch", [(i, (i & 4) | ((i + k) & 3)) for i in range(8)]) for k in range(1, 4)
+    ]
+    r_flip, l_quads = lax.optimization_barrier((r_flip, l_quads))
     r_pair = jnp.concatenate([right_block, r_flip], axis=0)
     quads = [r_pair] + [lax.ppermute(r_pair, "dap", [(i, (i + 4 * k) % 16) for i in range(16)]) for k in range(1, 4)]
     r_half = jnp.concatenate(quads, axis=0)
     r_other = lax.ppermute(r_half, "dap", [(i, i ^ 1) for i in range(16)])
+    place = jnp.stack([lax.axis_index("dap"), lax.axis_index("ch")]).astype(jnp.int32)
     out_weight, in_weight, in_gain, tri_gain, tri_weight = turned
-    place = lax.axis_index("dap").astype(jnp.int32).reshape(1)
-
     acts, pair_mid, normed = pl.pallas_call(
         pair_kernel,
         out_shape=(
@@ -290,15 +305,15 @@
             pltpu.VMEM((ROWS, LANES, LANES), BF16),
         ),
         in_specs=[pl.BlockSpec(memory_space=pltpu.SMEM)]
-        + [IN_VMEM] * 4
-        + [pl.BlockSpec(memory_space=pl.ANY)]
+        + [IN_VMEM] * 6
+        + [pl.BlockSpec(memory_space=pl.ANY)] * 2
         + [IN_VMEM] * 2,
         out_specs=(IN_VMEM,) * 3,
         scratch_shapes=[
             pltpu.VMEM((8, HIDDEN, 8, LANES), F32),
-            pltpu.VMEM((16, HIDDEN, 8, LANES), F32),
             pltpu.VMEM((ROWS * (HIDDEN + 8), LANES), F32),
             pltpu.VMEM((ROWS * HIDDEN, LANES), BF16),
+            pltpu.VMEM((16, HIDDEN, 8, LANES), F32),
             pltpu.VMEM((LANES, HIDDEN * LANES), BF16),
             pltpu.VMEM((1024, STEP_ROWS * LANES), BF16),
             pltpu.VMEM((1024, STEP_ROWS * LANES), BF16),
@@ -306,12 +321,14 @@
             pltpu.VMEM((LANES * PITCH, LANES), F32),
             pltpu.VMEM((LANES * PITCH, LANES), F32),
             pltpu.VMEM((LANES, 1024), BF16),
+            pltpu.VMEM((LANES, ROWS, LANES), BF16),
+            pltpu.SemaphoreType.DMA,
             pltpu.SemaphoreType.DMA,
         ],
-        compiler_params=pltpu.CompilerParams(vmem_limit_bytes=28 * MIB),
+        compiler_params=pltpu.CompilerParams(vmem_limit_bytes=32 * MIB),
         name="pair_update",
     )(
-        place, resident(l_all), resident(r_half), resident(r_other), resident(pair),
+        place, *[resident(x) for x in l_quads], resident(r_half), resident(r_other), in_hbm(pair),
         in_hbm(out_weight), resident(in_gain), resident(in_weight),
     )
     acts = lax.all_to_all(acts.reshape(LANES, LANES, LANES), both, 0, 0, tiled=True)

time: 160 us -> 155 us (0.969)
  starting transfers between devices: 19 us -> 26.9 us
  waiting for transfers between devices: 15 us -> 7.24 us
  blocking collectives: 97.7 us -> 95.3 us
  Pallas kernels: 26.6 us -> 24.4 us
    ppermute x0 -> x4, starting transfers between devices: none -> 11.5 us  [the longest x1 6.93 us: on_device(): lax.ppermute(left_block[None], 'ch', [(i, i ^ 4) for i in range(8)])]
    all_to_all x1 -> x0, waiting for transfers between devices: 7.32 us -> none  [on_device(): l_all = lax.all_to_all(left_blocks, 'ch', 0, 0, tiled=True)]
    all_to_all x1 -> x0, starting transfers between devices: 5.86 us -> none  [on_device(): l_all = lax.all_to_all(left_blocks, 'ch', 0, 0, tiled=True)]
    all_to_all x1, blocking collectives: 63 us -> 60.5 us  [on_device(): lax.all_to_all(acts.reshape(LANES, LANES, LANES), both, 0, 0, tiled=True)]
    pallas_call x1, Pallas kernels: 4.07 us -> 1.94 us  [on_device(): pl.pallas_call(operands_kernel, grid=(2,), out_shape=(jax.ShapeDtypeStruc...]
    ppermute x1, starting transfers between devices: 3.45 us -> 5.48 us  [on_device(): r_other = lax.ppermute(r_half, 'dap', [(i, i ^ 1) for i in range(16)])]
  transfers between devices with their start and end apart: 7 -> 10, of which waited for: 6 -> 7; matrix products, arithmetic and copies ran while one was open for 0% -> 0% of each run, Pallas kernels for 1% -> 1%
where the time goes in v3:
time: 155 us
  blocking collectives  95.3 us (61%)
  starting transfers between devices  26.9 us (17%)
  Pallas kernels  24.4 us (16%)
  waiting for transfers between devices  7.24 us (5%)
    all_to_all x1, blocking collectives, on_device(): lax.all_to_all(acts.reshape(LANES, LANES, LANES), both, 0, 0, tiled=True)  60.5 us
    all_to_all x1, blocking collectives, on_device(): tri = lax.all_to_all(tri, both, 0, 0, tiled=True)  34.7 us
    pallas_call x1, Pallas kernels, on_device(): pl.pallas_call(pair_kernel, out_shape=(pltpu.VMEM((LANES, 2, ROWS, LANES)...  14.1 us
    ppermute x1, starting transfers between devices, on_device(): lax.ppermute(left_block[None], 'ch', [(i, i ^ 4) for i in range(8)])  6.93 us
    ppermute x3, starting transfers between devices, on_device(): lax.ppermute(r_pair, 'dap', [(i, (i + 4 * k) % 16) for i in range(16)])  5.51 us
    ppermute x1, starting transfers between devices, on_device(): r_other = lax.ppermute(r_half, 'dap', [(i, i ^ 1) for i in range(16)])  5.48 us
    ppermute x3, starting transfers between devices, on_device(): lax.ppermute(l_pair, 'ch', [(i, i & 4 | i + k & 3) for i in range(8)])  4.54 us
    pallas_call x1, Pallas kernels, on_device(): pl.pallas_call(finish_kernel, grid=(ROWS // STEP_ROWS,), out_shape=jax.Sh...  4.5 us
  transfers between devices with their start and end apart: 10, of which 7 were waited for; matrix products, arithmetic and copies ran while one was open for 0% of the time, Pallas kernels for 1%

profile of v3, /device:TPU:1, one launch (start us, length us, event | category | flops | bytes accessed | tf_op | source)
XLA Modules:
  0.0 154.8 jit_solution(11389594739260104705)
XLA Ops:
  0.0 1.9 %operands.1 = (bf16[256,128]{1,0:T(8,128)(2,1)S(1)}, bf16[256,128]{1,0:T(8,128)(2,1)S(1)}) custom-call(bf16[2,8,64,256]{3,2,1,0:T(8,128)(2,1)} %bitcast.17, bf16[2,8,64,256]{3,2,1,0:T(8,128)(2,1)} %bitcast.18, s32[64,256]{1,0:T(8,128)} %keep.2, f32[1,256]{1,0:T(1,128)} %bitcast.20, bf16[64,256]{1,0:T(8,128)(2,1)} %bitcast.19), custom_call_target="tpu_custom_call" | custom-call | tf_op jit(solution)/shard_map/operands/pallas_call | solution.py:237
  1.9 0.7 collective-permute-start
  2.6 6.9 %collective-permute-start.1 = (bf16[1,256,128]{2,1,0:T(8,128)(2,1)S(1)}, bf16[1,256,128]{2,1,0:T(8,128)(2,1)S(1)}, u32[]{:S(2)}, u32[]{:S(2)}) collective-permute-start(bf16[1,256,128]{2,1,0:T(8,128)(2,1)S(1)} %bitcast.14), channel_id=1, source_target_pairs={{0,4},{1,5},{2,6},{3,7},{4,0},{5,1},{6,2},{7,3},{8,12},{9,13},{10,... | collective-permute-start | bytes 196616 | tf_op jit(solution)/shard_map/ppermute | solution.py:286
  9.5 1.5 weights.1
  11.0 0.0 copy-start
  11.1 0.7 copy-done
  11.7 0.0 collective-permute-done
  11.8 0.3 collective-permute-done.1
  12.1 3.9 %collective-permute-start.5 = (bf16[2,256,128]{2,1,0:T(8,128)(2,1)S(1)}, bf16[2,256,128]{2,1,0:T(8,128)(2,1)S(1)}, u32[]{:S(2)}, u32[]{:S(2)}) collective-permute-start(bf16[2,256,128]{2,1,0:T(8,128)(2,1)S(1)} %pad_maximum_fusion.l0), channel_id=1, source_target_pairs={{0,3},{1,0},{2,1},{3,2},{4,7},{5,4},{6,5},{7,6},{8,11},{9,8},{10,9... | collective-permute-start | bytes 393224 | tf_op jit(solution)/shard_map/ppermute | solution.py:291
  15.9 0.0 collective-permute-start.4
  15.9 0.7 collective-permute-start.3
  16.6 3.8 %collective-permute-start.2 = (bf16[1,256,128]{2,1,0:T(8,128)(2,1)S(1)}, bf16[1,256,128]{2,1,0:T(8,128)(2,1)S(1)}, u32[]{:S(2)}, u32[]{:S(2)}) collective-permute-start(bf16[1,256,128]{2,1,0:T(8,128)(2,1)S(1)} %collective-permute-done), channel_id=1, source_target_pairs={{0,16},{8,24},{16,0},{24,8},{32,48},{40,56},{48,32},{56,40},{64,80... | collective-permute-start | bytes 196616 | tf_op jit(solution)/shard_map/ppermute | solution.py:288
  20.4 1.6 %collective-permute-done.2 = bf16[1,256,128]{2,1,0:T(8,128)(2,1)S(1)} collective-permute-done((bf16[1,256,128]{2,1,0:T(8,128)(2,1)S(1)}, bf16[1,256,128]{2,1,0:T(8,128)(2,1)S(1)}, u32[]{:S(2)}, u32[]{:S(2)}) %collective-permute-start.2) | collective-permute-done | bytes 65568 | tf_op jit(solution)/shard_map/ppermute | solution.py:288
  22.0 0.0 collective-permute-done.5.l3
  22.0 0.0 collective-permute-done.4.l2
  22.0 0.4 collective-permute-done.3.l1
  22.4 2.1 %collective-permute-start.6 = (bf16[2,256,128]{2,1,0:T(8,128)(2,1)S(1)}, bf16[2,256,128]{2,1,0:T(8,128)(2,1)S(1)}, u32[]{:S(2)}, u32[]{:S(2)}) collective-permute-start(bf16[2,256,128]{2,1,0:T(8,128)(2,1)S(1)} %get-tuple-element.59), channel_id=1, source_target_pairs={{0,32},{8,40},{16,48},{24,56},{32,64},{40,72},{48,80},{56,88},{64,... | collective-permute-start | bytes 393224 | tf_op jit(solution)/shard_map/ppermute | solution.py:295
  24.5 2.8 %collective-permute-start.7 = (bf16[2,256,128]{2,1,0:T(8,128)(2,1)S(1)}, bf16[2,256,128]{2,1,0:T(8,128)(2,1)S(1)}, u32[]{:S(2)}, u32[]{:S(2)}) collective-permute-start(bf16[2,256,128]{2,1,0:T(8,128)(2,1)S(1)} %get-tuple-element.59), channel_id=1, source_target_pairs={{0,64},{8,72},{16,80},{24,88},{32,96},{40,104},{48,112},{56,120},{... | collective-permute-start | bytes 393224 | tf_op jit(solution)/shard_map/ppermute | solution.py:295
  27.3 0.6 collective-permute-start.8
  27.9 0.6 collective-permute-done.6
  28.5 2.6 %collective-permute-done.7 = bf16[2,256,128]{2,1,0:T(8,128)(2,1)S(1)} collective-permute-done((bf16[2,256,128]{2,1,0:T(8,128)(2,1)S(1)}, bf16[2,256,128]{2,1,0:T(8,128)(2,1)S(1)}, u32[]{:S(2)}, u32[]{:S(2)}) %collective-permute-start.7) | collective-permute-done | bytes 131104 | tf_op jit(solution)/shard_map/ppermute | solution.py:295
  31.1 0.3 collective-permute-done.8
  31.5 5.5 %collective-permute-start.9 = (bf16[8,256,128]{2,1,0:T(8,128)(2,1)S(1)}, bf16[8,256,128]{2,1,0:T(8,128)(2,1)S(1)}, u32[]{:S(2)}, u32[]{:S(2)}) collective-permute-start(bf16[8,256,128]{2,1,0:T(8,128)(2,1)S(1)} %constant_dynamic-update-slice_fusion.2.r_half), channel_id=1, source_target_pairs={{0,8},{8,0},{16,24},{24,16},{32,40},{40,32},{48,56},{56,48},{64,72... | collective-permute-start | bytes 1572872 | tf_op jit(solution)/shard_map/ppermute | solution.py:297
  36.9 0.1 pad_add_fusion.place
  37.0 1.5 collective-permute-done.9.r_other
  38.5 14.1 %pair_update.1 = (bf16[128,2,64,128]{3,2,1,0:T(8,128)(2,1)S(1)}, bf16[64,128,128]{2,1,0:T(8,128)(2,1)S(1)}, bf16[64,128,128]{2,1,0:T(8,128)(2,1)S(1)}) custom-call(s32[2]{0:T(128)S(1)} %pad_add_fusion.place, bf16[2,256,128]{2,1,0:T(8,128)(2,1)S(1)} %pad_maximum_fusion.l0, bf16[2,256,128]{2,1,0:T(8,128)(2,1)S(1)} %collective-permute-done.3.l1, ...), custom_call_target="tpu_custom_call" | custom-call | tf_op jit(solution)/shard_map/pair_update/pallas_call | solution.py:300
  52.6 60.5 %all_to_all.10 = bf16[128,128,128]{2,1,0:T(8,128)(2,1)S(1)} all-to-all(bf16[128,128,128]{2,1,0:T(8,128)(2,1)S(1)} %bitcast.13), channel_id=1, replica_groups=mesh['dap'=16,'ch'=8] {'dap','ch'}, dimensions={0} | all-to-all | bytes 8388608 | tf_op jit(solution)/shard_map/all_to_all | solution.py:334
  113.2 2.4 %triangle.1 = bf16[128,64,128]{2,1,0:T(8,128)(2,1)S(1)} custom-call(bf16[128,2,64,128]{3,2,1,0:T(8,128)(2,1)S(1)} %bitcast.12), custom_call_target="tpu_custom_call" | custom-call | tf_op jit(solution)/shard_map/triangle/pallas_call | solution.py:336
  115.5 0.0 copy-start.1
  115.5 34.7 %all_to_all.11.tri = bf16[128,64,128]{2,1,0:T(8,128)(2,1)S(1)} all-to-all(bf16[128,64,128]{2,1,0:T(8,128)(2,1)S(1)} %triangle.1), channel_id=1, replica_groups=mesh['dap'=16,'ch'=8] {'dap','ch'}, dimensions={0} | all-to-all | bytes 4194304 | tf_op jit(solution)/shard_map/all_to_all | solution.py:344
  150.3 0.0 copy-done.1
  150.3 4.5 %finish.1 = bf16[128,64,128]{2,1,0:T(8,128)(2,1)} custom-call(bf16[128,64,128]{2,1,0:T(8,128)(2,1)S(1)} %all_to_all.11.tri, bf16[64,128,128]{2,1,0:T(8,128)(2,1)S(1)} %get-tuple-element.55.mid, bf16[64,128,128]{2,1,0:T(8,128)(2,1)S(1)} %get-tuple-element.56.pair_normed, s32[128,128]{1,0:T(8,128)S(1)} %copy-done.1, f32[128,1]{1,0:T(8,128)S(1)} %get-tuple-element.57.gain, ...), custom_call_target="tpu_custom_call" | custom-call | tf_op jit(solution)/shard_map/finish/pallas_call | solution.py:346
  (6 shorter events, 0.1 us)
Async XLA Ops:
  1.9 9.8 %collective-permute-start = (bf16[1,256,128]{2,1,0:T(8,128)(2,1)S(1)}, bf16[1,256,128]{2,1,0:T(8,128)(2,1)S(1)}, u32[]{:S(2)}, u32[]{:S(2)}) collective-permute-start(bf16[1,256,128]{2,1,0:T(8,128)(2,1)S(1)} %bitcast.16), channel_id=1, source_target_pairs={{0,0},{1,16},{2,32},{3,48},{4,64},{5,80},{6,96},{7,112},{8,8},{9,2... | collective-permute-start | bytes 196616 | tf_op jit(solution)/shard_map/ppermute | solution.py:261
  2.6 9.4 %collective-permute-start.1 = (bf16[1,256,128]{2,1,0:T(8,128)(2,1)S(1)}, bf16[1,256,128]{2,1,0:T(8,128)(2,1)S(1)}, u32[]{:S(2)}, u32[]{:S(2)}) collective-permute-start(bf16[1,256,128]{2,1,0:T(8,128)(2,1)S(1)} %bitcast.14), channel_id=1, source_target_pairs={{0,4},{1,5},{2,6},{3,7},{4,0},{5,1},{6,2},{7,3},{8,12},{9,13},{10,... | collective-permute-start | bytes 196616 | tf_op jit(solution)/shard_map/ppermute | solution.py:286
  11.0 0.7 copy-start
  12.1 9.9 %collective-permute-start.5 = (bf16[2,256,128]{2,1,0:T(8,128)(2,1)S(1)}, bf16[2,256,128]{2,1,0:T(8,128)(2,1)S(1)}, u32[]{:S(2)}, u32[]{:S(2)}) collective-permute-start(bf16[2,256,128]{2,1,0:T(8,128)(2,1)S(1)} %pad_maximum_fusion.l0), channel_id=1, source_target_pairs={{0,3},{1,0},{2,1},{3,2},{4,7},{5,4},{6,5},{7,6},{8,11},{9,8},{10,9... | collective-permute-start | bytes 393224 | tf_op jit(solution)/shard_map/ppermute | solution.py:291
  15.9 6.1 %collective-permute-start.4 = (bf16[2,256,128]{2,1,0:T(8,128)(2,1)S(1)}, bf16[2,256,128]{2,1,0:T(8,128)(2,1)S(1)}, u32[]{:S(2)}, u32[]{:S(2)}) collective-permute-start(bf16[2,256,128]{2,1,0:T(8,128)(2,1)S(1)} %pad_maximum_fusion.l0), channel_id=1, source_target_pairs={{0,2},{1,3},{2,0},{3,1},{4,6},{5,7},{6,4},{7,5},{8,10},{9,11},{10,... | collective-permute-start | bytes 393224 | tf_op jit(solution)/shard_map/ppermute | solution.py:291
  15.9 6.4 %collective-permute-start.3 = (bf16[2,256,128]{2,1,0:T(8,128)(2,1)S(1)}, bf16[2,256,128]{2,1,0:T(8,128)(2,1)S(1)}, u32[]{:S(2)}, u32[]{:S(2)}) collective-permute-start(bf16[2,256,128]{2,1,0:T(8,128)(2,1)S(1)} %pad_maximum_fusion.l0), channel_id=1, source_target_pairs={{0,1},{1,2},{2,3},{3,0},{4,5},{5,6},{6,7},{7,4},{8,9},{9,10},{10,1... | collective-permute-start | bytes 393224 | tf_op jit(solution)/shard_map/ppermute | solution.py:291
  16.6 5.4 %collective-permute-start.2 = (bf16[1,256,128]{2,1,0:T(8,128)(2,1)S(1)}, bf16[1,256,128]{2,1,0:T(8,128)(2,1)S(1)}, u32[]{:S(2)}, u32[]{:S(2)}) collective-permute-start(bf16[1,256,128]{2,1,0:T(8,128)(2,1)S(1)} %collective-permute-done), channel_id=1, source_target_pairs={{0,16},{8,24},{16,0},{24,8},{32,48},{40,56},{48,32},{56,40},{64,80... | collective-permute-start | bytes 196616 | tf_op jit(solution)/shard_map/ppermute | solution.py:288
  22.4 6.1 %collective-permute-start.6 = (bf16[2,256,128]{2,1,0:T(8,128)(2,1)S(1)}, bf16[2,256,128]{2,1,0:T(8,128)(2,1)S(1)}, u32[]{:S(2)}, u32[]{:S(2)}) collective-permute-start(bf16[2,256,128]{2,1,0:T(8,128)(2,1)S(1)} %get-tuple-element.59), channel_id=1, source_target_pairs={{0,32},{8,40},{16,48},{24,56},{32,64},{40,72},{48,80},{56,88},{64,... | collective-permute-start | bytes 393224 | tf_op jit(solution)/shard_map/ppermute | solution.py:295
  24.5 6.6 %collective-permute-start.7 = (bf16[2,256,128]{2,1,0:T(8,128)(2,1)S(1)}, bf16[2,256,128]{2,1,0:T(8,128)(2,1)S(1)}, u32[]{:S(2)}, u32[]{:S(2)}) collective-permute-start(bf16[2,256,128]{2,1,0:T(8,128)(2,1)S(1)} %get-tuple-element.59), channel_id=1, source_target_pairs={{0,64},{8,72},{16,80},{24,88},{32,96},{40,104},{48,112},{56,120},{... | collective-permute-start | bytes 393224 | tf_op jit(solution)/shard_map/ppermute | solution.py:295
  27.3 4.1 %collective-permute-start.8 = (bf16[2,256,128]{2,1,0:T(8,128)(2,1)S(1)}, bf16[2,256,128]{2,1,0:T(8,128)(2,1)S(1)}, u32[]{:S(2)}, u32[]{:S(2)}) collective-permute-start(bf16[2,256,128]{2,1,0:T(8,128)(2,1)S(1)} %get-tuple-element.59), channel_id=1, source_target_pairs={{0,96},{8,104},{16,112},{24,120},{32,0},{40,8},{48,16},{56,24},{64... | collective-permute-start | bytes 393224 | tf_op jit(solution)/shard_map/ppermute | solution.py:295
  31.5 7.0 %collective-permute-start.9 = (bf16[8,256,128]{2,1,0:T(8,128)(2,1)S(1)}, bf16[8,256,128]{2,1,0:T(8,128)(2,1)S(1)}, u32[]{:S(2)}, u32[]{:S(2)}) collective-permute-start(bf16[8,256,128]{2,1,0:T(8,128)(2,1)S(1)} %constant_dynamic-update-slice_fusion.2.r_half), channel_id=1, source_target_pairs={{0,8},{8,0},{16,24},{24,16},{32,40},{40,32},{48,56},{56,48},{64,72... | collective-permute-start | bytes 1572872 | tf_op jit(solution)/shard_map/ppermute | solution.py:297
  115.5 34.8 %copy-start.1 = (s32[128,128]{1,0:T(8,128)S(1)}, s32[128,128]{1,0:T(8,128)}, u32[]{:S(2)}) copy-start(s32[128,128]{1,0:T(8,128)} %keep.3) | copy-start | bytes 196612

commit v4 on v3

--- a/solution.py
+++ b/solution.py
@@ -81,8 +81,8 @@
 
 def turn_left(place, quads, left, parts, rows):
     for k, blocks in enumerate(quads):
-        for q in range(2):
-            spot = ((place[1] & 4) | ((place[1] - k) & 3)) ^ (4 * q)
+        for q in range(4):
+            spot = ((place[1] & 4) | ((place[1] - q) & 3)) ^ (4 * k)
             parts[spot] = blocks[q].astype(F32).reshape(HIDDEN, 8, LANES)
     for c in range(HIDDEN):
         turned = parts[:, c].reshape(64, LANES).T
@@ -91,7 +91,7 @@
 
 
 def pair_kernel(
-    place, l0, l1, l2, l3, r_half, r_other, pair_far, out_weight, gain, in_weight,
+    place, l0, l1, r_half, r_other, pair_far, out_weight, gain, in_weight,
     acts, mid_out, normed_out,
     l_parts, l_rows, left, r_parts, right, outer_a, outer_b, pair_rows, left_rows, right_rows,
     weight_here, pair, weight_sem, pair_sem,
@@ -100,7 +100,7 @@
     fetch_pair = pltpu.make_async_copy(pair_far, pair, pair_sem)
     fetch_weight.start()
     fetch_pair.start()
-    turn_left(place, (l0, l1, l2, l3), left, l_parts, l_rows)
+    turn_left(place, (l0, l1), left, l_parts, l_rows)
     for q in range(8):
         for other, blocks in enumerate((r_half, r_other)):
             spot = (((place[0] ^ other) - 4 * (q // 2)) & 15) ^ (2 * (q % 2))
@@ -283,16 +283,18 @@
         compiler_params=pltpu.CompilerParams(vmem_limit_bytes=8 * MIB),
         name="weights",
     )(*[in_hbm(x) for x in raw[:5]])
-    l_flip = lax.ppermute(left_block[None], "ch", [(i, i ^ 4) for i in range(8)])
-    right_block, l_flip, turned = lax.optimization_barrier((right_block, l_flip, turned))
+    l_row = [left_block[None]] + [
+        lax.ppermute(left_block[None], "ch", [(i, (i & 4) | ((i + k) & 3)) for i in range(8)]) for k in range(1, 4)
+    ]
+    right_block, l_row, turned = lax.optimization_barrier((right_block, l_row, turned))
     r_flip = lax.ppermute(right_block, "dap", [(i, i ^ 2) for i in range(16)])
-    l_pair = jnp.concatenate([left_block[None], l_flip], axis=0)
-    l_quads = [l_pair] + [
-        lax.ppermute(l_pair, "ch", [(i, (i & 4) | ((i + k) & 3)) for i in range(8)]) for k in range(1, 4)
-    ]
-    r_flip, l_quads = lax.optimization_barrier((r_flip, l_quads))
+    l_own = jnp.concatenate(l_row, axis=0)
+    r_flip, l_own = lax.optimization_barrier((r_flip, l_own))
+    l_far = lax.ppermute(l_own, "ch", [(i, i ^ 4) for i in range(8)])
     r_pair = jnp.concatenate([right_block, r_flip], axis=0)
     quads = [r_pair] + [lax.ppermute(r_pair, "dap", [(i, (i + 4 * k) % 16) for i in range(16)]) for k in range(1, 4)]
+    quads, l_far = lax.optimization_barrier((quads, l_far))
+    l_quads = [l_own, l_far]
     r_half = jnp.concatenate(quads, axis=0)
     r_other = lax.ppermute(r_half, "dap", [(i, i ^ 1) for i in range(16)])
     place = jnp.stack([lax.axis_index("dap"), lax.axis_index("ch")]).astype(jnp.int32)
@@ -305,7 +307,7 @@
             pltpu.VMEM((ROWS, LANES, LANES), BF16),
         ),
         in_specs=[pl.BlockSpec(memory_space=pltpu.SMEM)]
-        + [IN_VMEM] * 6
+        + [IN_VMEM] * 4
         + [pl.BlockSpec(memory_space=pl.ANY)] * 2
         + [IN_VMEM] * 2,
         out_specs=(IN_VMEM,) * 3,

time: 155 us -> 152 us (0.981)
  waiting for transfers between devices: 7.24 us -> 12.6 us
  starting transfers between devices: 26.9 us -> 22.3 us
  blocking collectives: 95.3 us -> 92 us
    all_to_all x1, blocking collectives: 60.5 us -> 57.2 us  [on_device(): lax.all_to_all(acts.reshape(LANES, LANES, LANES), both, 0, 0, tiled=True)]
    ppermute x3, starting transfers between devices: 5.51 us -> 2.61 us  [on_device(): lax.ppermute(r_pair, 'dap', [(i, (i + 4 * k) % 16) for i in range(16)])]
    ppermute x1, starting transfers between devices: 3.75 us -> 1.21 us  [on_device(): r_flip = lax.ppermute(right_block, 'dap', [(i, i ^ 2) for i in range(16)])]
    ppermute x3, waiting for transfers between devices: 3.48 us -> 5.56 us  [on_device(): lax.ppermute(r_pair, 'dap', [(i, (i + 4 * k) % 16) for i in range(16)])]
    ppermute x1, waiting for transfers between devices: 1.64 us -> 3.37 us  [on_device(): r_flip = lax.ppermute(right_block, 'dap', [(i, i ^ 2) for i in range(16)])]
where the time goes in v4:
time: 152 us
  blocking collectives  92 us (61%)
  Pallas kernels  24.4 us (16%)
  starting transfers between devices  22.3 us (15%)
  waiting for transfers between devices  12.6 us (8%)
    all_to_all x1, blocking collectives, on_device(): lax.all_to_all(acts.reshape(LANES, LANES, LANES), both, 0, 0, tiled=True)  57.2 us
    all_to_all x1, blocking collectives, on_device(): tri = lax.all_to_all(tri, both, 0, 0, tiled=True)  34.7 us
    pallas_call x1, Pallas kernels, on_device(): pl.pallas_call(pair_kernel, out_shape=(pltpu.VMEM((LANES, 2, ROWS, LANES)...  14.1 us
    ppermute x3, starting transfers between devices, on_device(): lax.ppermute(left_block[None], 'ch', [(i, i & 4 | i + k & 3) for i in ran...  9.47 us
    ppermute x1, starting transfers between devices, on_device(): r_other = lax.ppermute(r_half, 'dap', [(i, i ^ 1) for i in range(16)])  6.26 us
    ppermute x3, waiting for transfers between devices, on_device(): lax.ppermute(r_pair, 'dap', [(i, (i + 4 * k) % 16) for i in range(16)])  5.56 us
    pallas_call x1, Pallas kernels, on_device(): pl.pallas_call(finish_kernel, grid=(ROWS // STEP_ROWS,), out_shape=jax.Sh...  4.5 us
    ppermute x1, waiting for transfers between devices, on_device(): r_flip = lax.ppermute(right_block, 'dap', [(i, i ^ 2) for i in range(16)])  3.37 us
  transfers between devices with their start and end apart: 10, of which 7 were waited for; matrix products, arithmetic and copies ran while one was open for 0% of the time, Pallas kernels for 1%

profile of v4, /device:TPU:1, one launch (start us, length us, event | category | flops | bytes accessed | tf_op | source)
XLA Modules:
  0.0 152.2 jit_solution(9114951869553114800)
XLA Ops:
  0.0 1.9 %operands.1 = (bf16[256,128]{1,0:T(8,128)(2,1)S(1)}, bf16[256,128]{1,0:T(8,128)(2,1)S(1)}) custom-call(bf16[2,8,64,256]{3,2,1,0:T(8,128)(2,1)} %bitcast.19, bf16[2,8,64,256]{3,2,1,0:T(8,128)(2,1)} %bitcast.20, s32[64,256]{1,0:T(8,128)} %keep.2, f32[1,256]{1,0:T(1,128)} %bitcast.22, bf16[64,256]{1,0:T(8,128)(2,1)} %bitcast.21), custom_call_target="tpu_custom_call" | custom-call | tf_op jit(solution)/shard_map/operands/pallas_call | solution.py:237
  1.9 0.7 collective-permute-start
  2.6 8.8 %collective-permute-start.3 = (bf16[1,256,128]{2,1,0:T(8,128)(2,1)S(1)}, bf16[1,256,128]{2,1,0:T(8,128)(2,1)S(1)}, u32[]{:S(2)}, u32[]{:S(2)}) collective-permute-start(bf16[1,256,128]{2,1,0:T(8,128)(2,1)S(1)} %bitcast.14), channel_id=1, source_target_pairs={{0,3},{1,0},{2,1},{3,2},{4,7},{5,4},{6,5},{7,6},{8,11},{9,8},{10,9... | collective-permute-start | bytes 196616 | tf_op jit(solution)/shard_map/ppermute | solution.py:287
  11.4 0.0 collective-permute-start.2
  11.4 0.7 collective-permute-start.1
  12.1 1.5 weights.1
  13.6 0.0 copy-start
  13.6 0.7 copy-done
  14.3 0.0 collective-permute-done
  14.3 0.0 collective-permute-done.3
  14.3 1.8 %collective-permute-done.2 = bf16[1,256,128]{2,1,0:T(8,128)(2,1)S(1)} collective-permute-done((bf16[1,256,128]{2,1,0:T(8,128)(2,1)S(1)}, bf16[1,256,128]{2,1,0:T(8,128)(2,1)S(1)}, u32[]{:S(2)}, u32[]{:S(2)}) %collective-permute-start.2) | collective-permute-done | bytes 65568 | tf_op jit(solution)/shard_map/ppermute | solution.py:287
  16.1 0.3 collective-permute-done.1
  16.5 1.2 collective-permute-start.4
  17.7 3.4 %collective-permute-done.4 = bf16[1,256,128]{2,1,0:T(8,128)(2,1)S(1)} collective-permute-done((bf16[1,256,128]{2,1,0:T(8,128)(2,1)S(1)}, bf16[1,256,128]{2,1,0:T(8,128)(2,1)S(1)}, u32[]{:S(2)}, u32[]{:S(2)}) %collective-permute-start.4) | collective-permute-done | bytes 65568 | tf_op jit(solution)/shard_map/ppermute | solution.py:290
  21.1 2.1 %collective-permute-start.8 = (bf16[4,256,128]{2,1,0:T(8,128)(2,1)S(1)}, bf16[4,256,128]{2,1,0:T(8,128)(2,1)S(1)}, u32[]{:S(2)}, u32[]{:S(2)}) collective-permute-start(bf16[4,256,128]{2,1,0:T(8,128)(2,1)S(1)} %pad_maximum_fusion.l0), channel_id=1, source_target_pairs={{0,4},{1,5},{2,6},{3,7},{4,0},{5,1},{6,2},{7,3},{8,12},{9,13},{10,... | collective-permute-start | bytes 786440 | tf_op jit(solution)/shard_map/ppermute | solution.py:293
  23.2 1.4 collective-permute-start.7
  24.6 1.2 collective-permute-start.6
  25.8 0.0 collective-permute-start.5
  25.8 1.3 collective-permute-done.7
  27.1 2.9 %collective-permute-done.6 = bf16[2,256,128]{2,1,0:T(8,128)(2,1)S(1)} collective-permute-done((bf16[2,256,128]{2,1,0:T(8,128)(2,1)S(1)}, bf16[2,256,128]{2,1,0:T(8,128)(2,1)S(1)}, u32[]{:S(2)}, u32[]{:S(2)}) %collective-permute-start.6) | collective-permute-done | bytes 131104 | tf_op jit(solution)/shard_map/ppermute | solution.py:295
  30.0 1.3 collective-permute-done.5
  31.4 0.0 collective-permute-done.8.l1
  31.5 6.3 %collective-permute-start.9 = (bf16[8,256,128]{2,1,0:T(8,128)(2,1)S(1)}, bf16[8,256,128]{2,1,0:T(8,128)(2,1)S(1)}, u32[]{:S(2)}, u32[]{:S(2)}) collective-permute-start(bf16[8,256,128]{2,1,0:T(8,128)(2,1)S(1)} %constant_dynamic-update-slice_fusion.2.r_half), channel_id=1, source_target_pairs={{0,8},{8,0},{16,24},{24,16},{32,40},{40,32},{48,56},{56,48},{64,72... | collective-permute-start | bytes 1572872 | tf_op jit(solution)/shard_map/ppermute | solution.py:299
  37.7 0.1 pad_add_fusion.place
  37.8 1.5 collective-permute-done.9.r_other
  39.3 14.1 %pair_update.1 = (bf16[128,2,64,128]{3,2,1,0:T(8,128)(2,1)S(1)}, bf16[64,128,128]{2,1,0:T(8,128)(2,1)S(1)}, bf16[64,128,128]{2,1,0:T(8,128)(2,1)S(1)}) custom-call(s32[2]{0:T(128)S(1)} %pad_add_fusion.place, bf16[4,256,128]{2,1,0:T(8,128)(2,1)S(1)} %pad_maximum_fusion.l0, bf16[4,256,128]{2,1,0:T(8,128)(2,1)S(1)} %collective-permute-done.8.l1, ...), custom_call_target="tpu_custom_call" | custom-call | tf_op jit(solution)/shard_map/pair_update/pallas_call | solution.py:302
  53.4 57.2 %all_to_all.10 = bf16[128,128,128]{2,1,0:T(8,128)(2,1)S(1)} all-to-all(bf16[128,128,128]{2,1,0:T(8,128)(2,1)S(1)} %bitcast.13), channel_id=1, replica_groups=mesh['dap'=16,'ch'=8] {'dap','ch'}, dimensions={0} | all-to-all | bytes 8388608 | tf_op jit(solution)/shard_map/all_to_all | solution.py:336
  110.6 2.4 %triangle.1 = bf16[128,64,128]{2,1,0:T(8,128)(2,1)S(1)} custom-call(bf16[128,2,64,128]{3,2,1,0:T(8,128)(2,1)S(1)} %bitcast.12), custom_call_target="tpu_custom_call" | custom-call | tf_op jit(solution)/shard_map/triangle/pallas_call | solution.py:338
  113.0 0.0 copy-start.1
  113.0 34.7 %all_to_all.11.tri = bf16[128,64,128]{2,1,0:T(8,128)(2,1)S(1)} all-to-all(bf16[128,64,128]{2,1,0:T(8,128)(2,1)S(1)} %triangle.1), channel_id=1, replica_groups=mesh['dap'=16,'ch'=8] {'dap','ch'}, dimensions={0} | all-to-all | bytes 4194304 | tf_op jit(solution)/shard_map/all_to_all | solution.py:346
  147.7 0.0 copy-done.1
  147.7 4.5 %finish.1 = bf16[128,64,128]{2,1,0:T(8,128)(2,1)} custom-call(bf16[128,64,128]{2,1,0:T(8,128)(2,1)S(1)} %all_to_all.11.tri, bf16[64,128,128]{2,1,0:T(8,128)(2,1)S(1)} %get-tuple-element.65.mid, bf16[64,128,128]{2,1,0:T(8,128)(2,1)S(1)} %get-tuple-element.66.pair_normed, s32[128,128]{1,0:T(8,128)S(1)} %copy-done.1, f32[128,1]{1,0:T(8,128)S(1)} %get-tuple-element.67.gain, ...), custom_call_target="tpu_custom_call" | custom-call | tf_op jit(solution)/shard_map/finish/pallas_call | solution.py:348
  (7 shorter events, 0.1 us)
Async XLA Ops:
  1.9 12.3 %collective-permute-start = (bf16[1,256,128]{2,1,0:T(8,128)(2,1)S(1)}, bf16[1,256,128]{2,1,0:T(8,128)(2,1)S(1)}, u32[]{:S(2)}, u32[]{:S(2)}) collective-permute-start(bf16[1,256,128]{2,1,0:T(8,128)(2,1)S(1)} %bitcast.18), channel_id=1, source_target_pairs={{0,0},{1,16},{2,32},{3,48},{4,64},{5,80},{6,96},{7,112},{8,8},{9,2... | collective-permute-start | bytes 196616 | tf_op jit(solution)/shard_map/ppermute | solution.py:261
  2.6 11.7 %collective-permute-start.3 = (bf16[1,256,128]{2,1,0:T(8,128)(2,1)S(1)}, bf16[1,256,128]{2,1,0:T(8,128)(2,1)S(1)}, u32[]{:S(2)}, u32[]{:S(2)}) collective-permute-start(bf16[1,256,128]{2,1,0:T(8,128)(2,1)S(1)} %bitcast.14), channel_id=1, source_target_pairs={{0,3},{1,0},{2,1},{3,2},{4,7},{5,4},{6,5},{7,6},{8,11},{9,8},{10,9... | collective-permute-start | bytes 196616 | tf_op jit(solution)/shard_map/ppermute | solution.py:287
  11.4 4.7 %collective-permute-start.2 = (bf16[1,256,128]{2,1,0:T(8,128)(2,1)S(1)}, bf16[1,256,128]{2,1,0:T(8,128)(2,1)S(1)}, u32[]{:S(2)}, u32[]{:S(2)}) collective-permute-start(bf16[1,256,128]{2,1,0:T(8,128)(2,1)S(1)} %bitcast.15), channel_id=1, source_target_pairs={{0,2},{1,3},{2,0},{3,1},{4,6},{5,7},{6,4},{7,5},{8,10},{9,11},{10,... | collective-permute-start | bytes 196616 | tf_op jit(solution)/shard_map/ppermute | solution.py:287
  11.4 5.0 %collective-permute-start.1 = (bf16[1,256,128]{2,1,0:T(8,128)(2,1)S(1)}, bf16[1,256,128]{2,1,0:T(8,128)(2,1)S(1)}, u32[]{:S(2)}, u32[]{:S(2)}) collective-permute-start(bf16[1,256,128]{2,1,0:T(8,128)(2,1)S(1)} %bitcast.16), channel_id=1, source_target_pairs={{0,1},{1,2},{2,3},{3,0},{4,5},{5,6},{6,7},{7,4},{8,9},{9,10},{10,1... | collective-permute-start | bytes 196616 | tf_op jit(solution)/shard_map/ppermute | solution.py:287
  13.6 0.7 copy-start
  16.5 4.6 %collective-permute-start.4 = (bf16[1,256,128]{2,1,0:T(8,128)(2,1)S(1)}, bf16[1,256,128]{2,1,0:T(8,128)(2,1)S(1)}, u32[]{:S(2)}, u32[]{:S(2)}) collective-permute-start(bf16[1,256,128]{2,1,0:T(8,128)(2,1)S(1)} %collective-permute-done), channel_id=1, source_target_pairs={{0,16},{8,24},{16,0},{24,8},{32,48},{40,56},{48,32},{56,40},{64,80... | collective-permute-start | bytes 196616 | tf_op jit(solution)/shard_map/ppermute | solution.py:290
  21.1 10.3 %collective-permute-start.8 = (bf16[4,256,128]{2,1,0:T(8,128)(2,1)S(1)}, bf16[4,256,128]{2,1,0:T(8,128)(2,1)S(1)}, u32[]{:S(2)}, u32[]{:S(2)}) collective-permute-start(bf16[4,256,128]{2,1,0:T(8,128)(2,1)S(1)} %pad_maximum_fusion.l0), channel_id=1, source_target_pairs={{0,4},{1,5},{2,6},{3,7},{4,0},{5,1},{6,2},{7,3},{8,12},{9,13},{10,... | collective-permute-start | bytes 786440 | tf_op jit(solution)/shard_map/ppermute | solution.py:293
  23.2 3.9 %collective-permute-start.7 = (bf16[2,256,128]{2,1,0:T(8,128)(2,1)S(1)}, bf16[2,256,128]{2,1,0:T(8,128)(2,1)S(1)}, u32[]{:S(2)}, u32[]{:S(2)}) collective-permute-start(bf16[2,256,128]{2,1,0:T(8,128)(2,1)S(1)} %constant_dynamic-update-slice_fusion), channel_id=1, source_target_pairs={{0,96},{8,104},{16,112},{24,120},{32,0},{40,8},{48,16},{56,24},{64... | collective-permute-start | bytes 393224 | tf_op jit(solution)/shard_map/ppermute | solution.py:295
  24.6 5.4 %collective-permute-start.6 = (bf16[2,256,128]{2,1,0:T(8,128)(2,1)S(1)}, bf16[2,256,128]{2,1,0:T(8,128)(2,1)S(1)}, u32[]{:S(2)}, u32[]{:S(2)}) collective-permute-start(bf16[2,256,128]{2,1,0:T(8,128)(2,1)S(1)} %constant_dynamic-update-slice_fusion), channel_id=1, source_target_pairs={{0,64},{8,72},{16,80},{24,88},{32,96},{40,104},{48,112},{56,120},{... | collective-permute-start | bytes 393224 | tf_op jit(solution)/shard_map/ppermute | solution.py:295
  25.8 5.6 %collective-permute-start.5 = (bf16[2,256,128]{2,1,0:T(8,128)(2,1)S(1)}, bf16[2,256,128]{2,1,0:T(8,128)(2,1)S(1)}, u32[]{:S(2)}, u32[]{:S(2)}) collective-permute-start(bf16[2,256,128]{2,1,0:T(8,128)(2,1)S(1)} %constant_dynamic-update-slice_fusion), channel_id=1, source_target_pairs={{0,32},{8,40},{16,48},{24,56},{32,64},{40,72},{48,80},{56,88},{64,... | collective-permute-start | bytes 393224 | tf_op jit(solution)/shard_map/ppermute | solution.py:295
  31.5 7.8 %collective-permute-start.9 = (bf16[8,256,128]{2,1,0:T(8,128)(2,1)S(1)}, bf16[8,256,128]{2,1,0:T(8,128)(2,1)S(1)}, u32[]{:S(2)}, u32[]{:S(2)}) collective-permute-start(bf16[8,256,128]{2,1,0:T(8,128)(2,1)S(1)} %constant_dynamic-update-slice_fusion.2.r_half), channel_id=1, source_target_pairs={{0,8},{8,0},{16,24},{24,16},{32,40},{40,32},{48,56},{56,48},{64,72... | collective-permute-start | bytes 1572872 | tf_op jit(solution)/shard_map/ppermute | solution.py:299
  113.0 34.8 %copy-start.1 = (s32[128,128]{1,0:T(8,128)S(1)}, s32[128,128]{1,0:T(8,128)}, u32[]{:S(2)}) copy-start(s32[128,128]{1,0:T(8,128)} %keep.3) | copy-start | bytes 196612
